TPU v7x, 32 devices: a whole 2x2x4 slice. The times are simulated.
32 devices in a mesh: gx: 8 (over z, x), gy: 4 (over y, core).
Axes of the slice: x: 2, y: 2, z: 4, core: 2. Of those that a mesh axis runs over, the one named last changes fastest.
Arguments:
- resident_rows: int32 [4, 8, 32768], P('gy', 'gx'), may hold values from 0 to 1023
- resident_columns: int32 [4, 8, 32768], P('gy', 'gx'), may hold values from 0 to 511
- resident_strength: float32 [3, 4, 8, 32768], P(None, 'gy', 'gx'), may hold values from -6 to 6
- crossing_rows: int32 [4, 8, 2048], P('gy', 'gx'), may hold values from 0 to 1023
- crossing_columns: int32 [4, 8, 2048], P('gy', 'gx'), may hold values from 0 to 511
- crossing_strength: float32 [3, 4, 8, 2048], P(None, 'gy', 'gx'), may hold values from -6 to 6
- crossing_count: int32 [4, 8], P('gy', 'gx'), may hold values from 512 to 2048, as said below
Outputs:
- vorticity_spectrum: float32 [2, 3, 1, 4096, 4096], P(None, None, None, 'gy', 'gx')
Inputs may be any that keep to these rules, and one draw needn't show every extreme that they name: `crossing_count`: in every draw at least one device has exactly 2048 live send slots.
All inputs are finite; a program needn't handle non-finite values.
Results may differ from a plain program's by a relative error of at most 0.0003.
Values sent between devices are 32-bit elements; how exact they have to be, the bound alone decides.
No kernel may reach another device: no remote copies, remote signals or barrier semaphores. Data moves between devices by JAX's collectives and lax.ppermute only.
A program may use at most 192 MiB of HBM per device.

v0:
```python
import math

import jax
import jax.numpy as jnp
import ml_dtypes
import numpy as np
from jax import lax
from jax.experimental import pallas as pl
from jax.experimental.pallas import tpu as pltpu
from jax.sharding import PartitionSpec as P

NX = 4096
NY = 4096
LEV = 1


TWO_PI = 2.0 * math.pi

BIN_ROWS = 256
BIN_COLS = 32
CHUNK = 640
GROUP = 2

F8 = jnp.float8_e4m3fn
PIECES = 3
STEP = 16.0
TOP = 384.0
LANES = 128


def from_behind(value, axis, steps):
    count = lax.axis_size(axis)
    pairs = [(source, (source + steps) % count) for source in range(count)]
    return lax.ppermute(value, axis, pairs)


def flip(value, axis, mask):
    count = lax.axis_size(axis)
    return lax.ppermute(value, axis, [(source, source ^ mask) for source in range(count)])


def bit_reverse(slab_index, bit_count):
    result = jnp.zeros_like(slab_index)
    for level in range(bit_count):
        result = result | (slab_index >> level & 1) << bit_count - 1 - level
    return result


def partner_2(block, axis, stride):
    count = lax.axis_size(axis)
    route = []
    for low in range(count):
        high = low | 1 << stride
        if high != low and high < count:
            route += [(low, high), (high, low)]
    return lax.ppermute(block, axis, route)


def section_mix(parts, partner, slab_index, bit_number):
    half_span = 1 << bit_number
    upper_half = slab_index >> bit_number & 1 == 1
    phase_angle = (slab_index & half_span - 1).astype(jnp.float32) * (-math.pi / half_span)
    cosine = jnp.cos(phase_angle)
    sine_value = jnp.sin(phase_angle)
    summed = parts + partner
    difference = partner - parts
    if parts.shape[0] == 1:
        summed = jnp.concatenate([summed, jnp.zeros_like(summed)])
        turned = jnp.concatenate([difference * cosine, difference * sine_value])
    else:
        turned = jnp.stack(
            [
                difference[0] * cosine - difference[1] * sine_value,
                difference[0] * sine_value + difference[1] * cosine,
            ]
        )
    return jnp.where(upper_half, turned, summed)


def local_table(k_first, slab_count, length):
    total = slab_count * length
    row_index = lax.broadcasted_iota(jnp.int32, (length, length), 0)
    col_index = lax.broadcasted_iota(jnp.int32, (length, length), 1)
    phase = col_index * (k_first + slab_count * row_index) % total
    phase_angle = phase.astype(jnp.float32) * (TWO_PI / total)
    return (jnp.cos(phase_angle), -jnp.sin(phase_angle))


def along(parts, table_real, table_imag, spec):
    def product(data, table):
        return jnp.einsum(
            spec,
            data,
            table,
            precision=lax.Precision.HIGHEST,
            preferred_element_type=jnp.float32,
        )

    return jnp.stack(
        [
            product(parts[0], table_real) - product(parts[1], table_imag),
            product(parts[0], table_imag) + product(parts[1], table_real),
        ]
    )


def dense_shards(
    resident_rows,
    resident_columns,
    resident_strength,
    crossing_rows,
    crossing_columns,
    crossing_strength,
    crossing_count,
):
    cells_x = NX // lax.axis_size("gx")
    cells_y = NY // lax.axis_size("gy")
    slot_count = crossing_rows.shape[-1]
    slot_index = lax.broadcasted_iota(jnp.int32, (1, slot_count), 1)
    live_slot = (slot_index < crossing_count).astype(jnp.float32)
    outgoing = jnp.concatenate(
        [
            crossing_rows.reshape(1, slot_count).astype(jnp.float32),
            crossing_columns.reshape(1, slot_count).astype(jnp.float32),
            crossing_strength.reshape(3, slot_count) * live_slot,
        ],
        axis=0,
    )
    arrived = from_behind(outgoing, "gx", 1)
    resident_ids = resident_rows.reshape(-1) * cells_x + resident_columns.reshape(-1)
    arrived_ids = arrived[0].astype(jnp.int32) * cells_x + arrived[1].astype(jnp.int32)
    cell_ids = jnp.concatenate([resident_ids, arrived_ids])
    weights = jnp.concatenate([resident_strength.reshape(3, -1), arrived[2:]], axis=1)
    cell_total = LEV * cells_y * cells_x
    deposited = jnp.stack(
        [
            jax.ops.segment_sum(weights[component], cell_ids, num_segments=cell_total)
            for component in range(3)
        ]
    )
    vorticity = deposited.reshape(1, 3, LEV, cells_y, cells_x) * (1.0 / math.sqrt(NX * NY))
    parts = vorticity
    for axis, cells, spec in (
        ("gx", cells_x, "clyx,kx->clyk"),
        ("gy", cells_y, "clyx,ky->clkx"),
    ):
        bits = lax.axis_size(axis).bit_length() - 1
        slab_index = lax.axis_index(axis)
        for bit_number in range(bits - 1, -1, -1):
            partner = partner_2(parts, axis, bit_number)
            parts = section_mix(parts, partner, slab_index, bit_number)
        table_real, table_imag = local_table(bit_reverse(slab_index, bits), 1 << bits, cells)
        parts = along(parts, table_real, table_imag, spec)
    return parts


def bin_key(rows, columns, cells_x):
    column = (columns & 1) * (cells_x // 2) + (columns >> 1)
    bin_index = (column // BIN_COLS) * 4 + (rows & 3)
    return bin_index * (BIN_ROWS * BIN_COLS) + (rows >> 2) * BIN_COLS + column % BIN_COLS


def deposit(sources, signs, cells_x, cells_y, residents, base_mesh, after):
    count = len(sources)
    row_bins = cells_y // BIN_ROWS
    group_bins = row_bins * GROUP
    width = sources[0].shape[-1]
    first_start = width - LANES
    arrivals = first_start - residents
    window = CHUNK + LANES
    shift = BIN_COLS.bit_length() - 1
    based = base_mesh is not None

    def kernel(signs_ref, *refs):
        source_refs = refs[:count]
        base_ref = refs[count] if based else None
        out_ref, starts_ref, sems = refs[-3:]
        group = pl.program_id(0)

        @pl.when(group == 0)
        def _():
            copies = [
                pltpu.make_async_copy(
                    source_refs[s].at[:, pl.ds(first_start, LANES)],
                    starts_ref.at[s],
                    sems.at[s],
                )
                for s in range(count)
            ]
            for copy in copies:
                copy.start()
            for copy in copies:
                copy.wait()

        scale, unscale = starts_ref[0, 2, 0], starts_ref[0, 3, 0]
        for s in range(1, count):
            scale = jnp.minimum(scale, starts_ref[s, 2, 0])
            unscale = jnp.maximum(unscale, starts_ref[s, 3, 0])
        spans = []
        steps = jnp.int32(0)
        for b in range(group_bins):
            bin_index = group * group_bins + b
            for s in range(count):
                begin, begin_2 = (starts_ref[s, i, bin_index].astype(jnp.int32) for i in (0, 1))
                end, end_2 = (starts_ref[s, i, bin_index + 1].astype(jnp.int32) for i in (0, 1))
                length, length_2 = end - begin, end_2 - begin_2
                spans.append((begin, length, begin_2, length_2))
                steps = jnp.maximum(steps, (length + length_2 + CHUNK - 1) // CHUNK)
                steps = jnp.maximum(steps, (length_2 + LANES - 1) // LANES)
        lane = lax.broadcasted_iota(jnp.int32, (1, CHUNK), 1)
        tail_lane = lax.broadcasted_iota(jnp.int32, (1, LANES), 1)

        def ramp(length):
            return (
                lax.broadcasted_iota(jnp.int32, (length, CHUNK), 0)
                .astype(jnp.float32)
                .astype(jnp.bfloat16)
            )

        row_ramp, col_ramp = ramp(BIN_ROWS), ramp(BIN_COLS)
        one, zero = jnp.bfloat16(1), jnp.bfloat16(0)

        def rolled(source_ref, place, low, high, size, lead):
            offset = low + jnp.minimum((place - low) // LANES * LANES, high - low - size)
            block = source_ref[:, pl.ds(pl.multiple_of(offset, LANES), size)]
            return pltpu.roll(block, lax.rem(2 * size + lead - (place - offset), size), 1)

        def bin_total(step, b):
            base = (group * group_bins + b) * (BIN_ROWS * BIN_COLS)
            hits, weights = [], []
            for s in range(count):
                begin, length, begin_2, length_2 = spans[b * count + s]
                done_2 = jnp.minimum(length_2, step * LANES)
                now_2 = jnp.minimum(length_2 - done_2, LANES)
                done = jnp.minimum(length, step * CHUNK - done_2)
                now = jnp.minimum(length - done, CHUNK - now_2)
                block = rolled(source_refs[s], begin + done, 0, residents, window, 0)[:, :CHUNK]
                tail = rolled(
                    source_refs[s],
                    residents + begin_2 + done_2,
                    residents,
                    residents + arrivals,
                    2 * LANES,
                    LANES - now_2,
                )[:, :LANES]
                tail = jnp.where(tail_lane >= LANES - now_2, tail, block[:, CHUNK - LANES :])
                block = jnp.concatenate([block[:, : CHUNK - LANES], tail], axis=1)
                local = block[0:1].astype(jnp.int32) - base
                row = jnp.where(
                    (lane < now) | (lane >= CHUNK - now_2),
                    lax.shift_right_arithmetic(local, shift),
                    -1,
                )
                col = local & (BIN_COLS - 1)
                row = row.astype(jnp.float32).astype(jnp.bfloat16)
                col = col.astype(jnp.float32).astype(jnp.bfloat16)
                hits.append(jnp.where(row_ramp == row, one, zero).astype(F8))
                mask = col_ramp == col
                pieces, rest = [], block * (signs_ref[s] * scale)
                for _ in range(PIECES):
                    piece = rest.astype(F8).astype(jnp.float32)
                    pieces.append(piece.astype(jnp.bfloat16))
                    rest = (rest - piece) * STEP
                weights.append(
                    jnp.concatenate(
                        [
                            jnp.where(
                                mask,
                                jnp.broadcast_to(piece[k : k + 1], (BIN_COLS, CHUNK)),
                                zero,
                            )
                            for piece in pieces
                            for k in (1, 2, 3)
                        ],
                        axis=0,
                    ).astype(F8)
                )
            total = lax.dot_general(
                jnp.concatenate(weights, axis=1),
                jnp.concatenate(hits, axis=1),
                (((1,), (1,)), ((), ())),
                preferred_element_type=jnp.float32,
            )
            total = total.reshape(PIECES, 3, BIN_COLS, BIN_ROWS)
            result = total[PIECES - 1]
            for piece in range(PIECES - 2, -1, -1):
                result = result * (1.0 / STEP) + total[piece]
            return result * unscale

        def cells_of(b):
            col_bin, row_bin = b // row_bins, b % row_bins
            return (
                slice(None),
                slice(col_bin * BIN_COLS, (col_bin + 1) * BIN_COLS),
                slice(row_bin * BIN_ROWS, (row_bin + 1) * BIN_ROWS),
            )

        def body(step, carry):
            totals = [bin_total(step, b) for b in range(group_bins)]
            for b in range(group_bins):
                out_ref[cells_of(b)] += totals[b]
            return carry

        for b in range(group_bins):
            total = bin_total(0, b)
            out_ref[cells_of(b)] = total + base_ref[cells_of(b)] if based else total
        lax.fori_loop(1, steps, body, 0)

    flops = count * width * BIN_ROWS * BIN_COLS * 24
    out_spec = pl.BlockSpec((3, GROUP * BIN_COLS, cells_y), lambda g: (0, g, 0))
    return pl.pallas_call(
        kernel,
        grid=(cells_x // (GROUP * BIN_COLS),),
        in_specs=[pl.BlockSpec(memory_space=pltpu.SMEM)]
        + [pl.BlockSpec(memory_space=pltpu.VMEM)] * count
        + [out_spec] * based
        + [pl.BlockSpec(memory_space=pl.ANY)] * len(after),
        out_specs=out_spec,
        out_shape=jax.ShapeDtypeStruct((3, cells_x, cells_y), jnp.float32),
        scratch_shapes=[
            pltpu.SMEM((count, 4, LANES), jnp.float32),
            pltpu.SemaphoreType.DMA((count,)),
        ],
        compiler_params=pltpu.CompilerParams(vmem_limit_bytes=10 << 20),
        cost_estimate=pl.CostEstimate(
            flops=flops, bytes_accessed=12 * cells_x * cells_y, transcendentals=0
        ),
        name="deposit",
    )(signs, *sources, *([base_mesh] if based else []), *after)


def turns(numerator, total):
    angle = (numerator % total).astype(jnp.float32) * (TWO_PI / total)
    return jnp.cos(angle), -jnp.sin(angle)


def stage_table(radix, length):
    k = np.arange(length)[None, :, None]
    n = radix * np.arange(length)[None, None, :] + np.arange(radix)[:, None, None]
    angle = (k * n % (radix * length)) * (-TWO_PI / (radix * length))
    real, imag = np.cos(angle), np.sin(angle)
    table = np.concatenate(
        [np.concatenate([real, -imag], axis=2), np.concatenate([imag, real], axis=2)], axis=1
    )
    high = table.astype(ml_dtypes.bfloat16)
    low = (table - high.astype(np.float64)).astype(ml_dtypes.bfloat16)
    return jnp.asarray(np.concatenate([high, high, low], axis=2))


def phases(k_first, radix, length, total):
    place = lax.iota(jnp.int32, radix * length)
    return turns(k_first * (radix * (place % length) + place // length), total)


def split(value):
    high = value.astype(jnp.bfloat16)
    return high, (value - high.astype(jnp.float32)).astype(jnp.bfloat16)


def columns_transform(meshes, scalars, phase, held, component, block):
    count = len(meshes)
    cells_x, cells_y = meshes[0].shape[1:]
    half = cells_x // 2

    def kernel(scalars_ref, phase_ref, held_ref, *refs):
        mesh_refs, out_ref = refs[:count], refs[count]
        lanes = pl.ds(pl.multiple_of(pl.program_id(0) * block, LANES), block)
        pieces = []
        for residue in range(2):
            rows = slice(residue * half, (residue + 1) * half)
            data = [mesh_ref[component, rows, lanes] for mesh_ref in mesh_refs]
            real = sum(scalars_ref[0, i] * data[i] for i in range(count))
            imag = sum(scalars_ref[1, i] * data[i] for i in range(count))
            cosine, sine = (
                jnp.concatenate([phase_ref[i, rows, :]] * (block // LANES), axis=1) for i in (0, 1)
            )
            real, imag = real * cosine - imag * sine, real * sine + imag * cosine
            high, low = split(jnp.concatenate([real, imag], axis=0))
            pieces.append(
                jnp.dot(
                    held_ref[residue],
                    jnp.concatenate([high, low, high], axis=0),
                    preferred_element_type=jnp.float32,
                )
            )
        for part in range(2):
            rows = slice(part * half, (part + 1) * half)
            out_ref[part, 0, :half] = pieces[0][rows] + pieces[1][rows]
            out_ref[part, 0, half:] = pieces[0][rows] - pieces[1][rows]

    return pl.pallas_call(
        kernel,
        grid=(cells_y // block,),
        in_specs=[
            pl.BlockSpec(memory_space=pltpu.SMEM),
            pl.BlockSpec(memory_space=pltpu.VMEM),
            pl.BlockSpec(memory_space=pltpu.VMEM),
        ]
        + [pl.BlockSpec(memory_space=pltpu.VMEM)] * count,
        out_specs=pl.BlockSpec((2, 1, cells_x, block), lambda g: (0, 0, 0, g)),
        out_shape=jax.ShapeDtypeStruct((2, 1, cells_x, cells_y), jnp.float32),
        compiler_params=pltpu.CompilerParams(vmem_limit_bytes=14 << 20),
        cost_estimate=pl.CostEstimate(
            flops=12 * cells_x * cells_x * cells_y,
            bytes_accessed=(count + 2) * 4 * cells_x * cells_y,
            transcendentals=0,
        ),
        name="columns_transform",
    )(scalars, phase, held, *meshes)


def rows_transform(own, partner, scalars, held, block, component, count, result):
    cells_x, cells_y = own.shape[2:]
    quarter = cells_y // 4

    def kernel(scalars_ref, held_ref, own_ref, partner_ref, *refs):
        out_ref = refs[-1]
        pieces = []
        for residue in range(4):
            where = slice(residue * quarter, (residue + 1) * quarter)
            own_real, own_imag = scalars_ref[0:1, where], scalars_ref[1:2, where]
            other_real, other_imag = scalars_ref[2:3, where], scalars_ref[3:4, where]
            a, b = own_ref[0, 0, :, where], own_ref[1, 0, :, where]
            d, e = partner_ref[0, 0, :, where], partner_ref[1, 0, :, where]
            real = own_real * a - own_imag * b + other_real * d - other_imag * e
            imag = own_real * b + own_imag * a + other_real * e + other_imag * d
            high, low = split(jnp.concatenate([real, imag], axis=1))
            piece = lax.dot_general(
                held_ref[residue],
                jnp.concatenate([high, low, high], axis=1),
                (((1,), (1,)), ((), ())),
                preferred_element_type=jnp.float32,
            )
            pieces.append((piece[:quarter], piece[quarter:]))
        (ar, ai), (br, bi), (cr, ci), (dr, di) = pieces
        even_r, even_i, odd_r, odd_i = ar + cr, ai + ci, br + dr, bi + di
        diff_r, diff_i, turn_r, turn_i = ar - cr, ai - ci, br - dr, bi - di
        out_ref[0, 0, 0, 0 * quarter : 1 * quarter] = even_r + odd_r
        out_ref[1, 0, 0, 0 * quarter : 1 * quarter] = even_i + odd_i
        out_ref[0, 0, 0, 1 * quarter : 2 * quarter] = diff_r + turn_i
        out_ref[1, 0, 0, 1 * quarter : 2 * quarter] = diff_i - turn_r
        out_ref[0, 0, 0, 2 * quarter : 3 * quarter] = even_r - odd_r
        out_ref[1, 0, 0, 2 * quarter : 3 * quarter] = even_i - odd_i
        out_ref[0, 0, 0, 3 * quarter : 4 * quarter] = diff_r - turn_i
        out_ref[1, 0, 0, 3 * quarter : 4 * quarter] = diff_i + turn_r

    spec = pl.BlockSpec((2, 1, block, cells_y), lambda g: (0, 0, g, 0))
    chained = result is not None
    return pl.pallas_call(
        kernel,
        grid=(cells_x // block,),
        in_specs=[
            pl.BlockSpec(memory_space=pltpu.VMEM),
            pl.BlockSpec(memory_space=pltpu.VMEM),
            spec,
            spec,
        ]
        + [pl.BlockSpec(memory_space=pl.ANY)] * chained,
        out_specs=pl.BlockSpec(
            (2, 1, 1, cells_y, block), lambda g: (0, component, 0, 0, g)
        ),
        out_shape=jax.ShapeDtypeStruct((2, count, 1, cells_y, cells_x), jnp.float32),
        input_output_aliases={4: 0} if chained else {},
        compiler_params=pltpu.CompilerParams(vmem_limit_bytes=24 << 20),
        cost_estimate=pl.CostEstimate(
            flops=6 * cells_y * cells_y * cells_x,
            bytes_accessed=24 * cells_x * cells_y,
            transcendentals=0,
        ),
        name="rows_transform",
    )(scalars, held, own, partner, *([result] if chained else []))


def particle_shards(
    resident_rows,
    resident_columns,
    resident_strength,
    crossing_rows,
    crossing_columns,
    crossing_strength,
    crossing_count,
):
    cells_x = NX // lax.axis_size("gx")
    cells_y = NY // lax.axis_size("gy")
    bins = (cells_y // BIN_ROWS) * (cells_x // BIN_COLS)
    gx, gy = lax.axis_index("gx"), lax.axis_index("gy")
    x, z = gx & 1, gx >> 1
    core, y = gy & 1, gy >> 1
    kx_first = bit_reverse(gx, 3)
    ky_first = bit_reverse(gy, 2)

    bin_cells = BIN_ROWS * BIN_COLS
    slot_count = crossing_rows.shape[-1]
    live_slot = lax.iota(jnp.int32, slot_count) < crossing_count.reshape(1)
    key = bin_key(crossing_rows.reshape(-1), crossing_columns.reshape(-1), cells_x)
    key = jnp.where(live_slot, key, bins * bin_cells)
    outgoing = lax.sort(
        (key, *(jnp.where(live_slot, crossing_strength[i].reshape(-1), 0.0) for i in range(3))),
        num_keys=1,
        is_stable=False,
    )
    outgoing = jnp.stack([outgoing[0].astype(jnp.float32), *outgoing[1:]])
    arrived = from_behind(outgoing, "gx", 1)
    key = bin_key(resident_rows.reshape(-1), resident_columns.reshape(-1), cells_x)
    residents = key.shape[0]
    key, *strength = lax.sort(
        (key, *(resident_strength[i].reshape(-1) for i in range(3))), num_keys=1, is_stable=False
    )
    bounds = lax.broadcasted_iota(jnp.int32, (LANES, 1), 0) * bin_cells
    starts = jnp.sum((key[None, :] < bounds).astype(jnp.float32), axis=1)
    starts_2 = jnp.sum((arrived[0:1] < bounds.astype(jnp.float32)).astype(jnp.float32), axis=1)
    largest = jnp.maximum(jnp.max(jnp.abs(resident_strength)), jnp.max(jnp.abs(arrived[1:])))
    largest = jnp.maximum(largest, 1e-30)
    particles = jnp.concatenate(
        [
            jnp.stack([key.astype(jnp.float32), *strength]),
            arrived,
            jnp.stack(
                [
                    starts,
                    starts_2,
                    jnp.broadcast_to(TOP / largest, (LANES,)),
                    jnp.broadcast_to(largest / TOP, (LANES,)),
                ]
            ),
        ],
        axis=1,
    )

    held_x, held_y = stage_table(2, cells_x // 2), stage_table(4, cells_y // 4)
    kx_low = kx_first & 3

    def signs(members):
        values = []
        for side, k in members:
            slab_y = y if side is near else 1 - y
            flips = kx_low * ((z ^ (k >> 1)) >> 1) + y * slab_y
            values.append((1 - 2 * (flips & 1)).astype(jnp.float32))
        return jnp.stack(values)

    near, far, meshes = {0: particles}, {}, {}
    last = []

    def add(*members):
        sources = [side[k] for side, k in members]
        kind = members[0][1] & 3
        meshes[kind] = deposit(
            sources, signs(members), cells_x, cells_y, residents, meshes.get(kind), last
        )
        last[:] = [meshes[kind]]
        hold.kind = kind

    def hold(*moved):
        held = lax.optimization_barrier([last[0]] + [side[k] for side, k in moved])
        last[0] = held[0]
        meshes[hold.kind] = held[0]
        for (side, k), value in zip(moved, held[1:]):
            side[k] = value

    far[0] = flip(near[0], "gy", 2)
    near[1] = flip(near[0], "gx", 1)
    near[4] = flip(near[0], "gx", 4)
    near[2] = flip(near[0], "gx", 2)
    add((near, 0))
    hold((near, 1))
    far[1] = flip(near[1], "gy", 2)
    add((far, 0))
    hold((near, 4), (near, 2))
    far[4] = flip(near[4], "gy", 2)
    near[5] = flip(near[4], "gx", 1)
    near[6] = flip(near[4], "gx", 2)
    far[2] = flip(near[2], "gy", 2)
    near[3] = flip(near[2], "gx", 1)
    add((near, 1), (far, 1))
    hold((far, 4), (near, 5), (near, 6), (near, 3), (far, 2))
    far[5] = flip(far[4], "gx", 1)
    far[6] = flip(near[6], "gy", 2)
    near[7] = flip(near[6], "gx", 1)
    add((near, 4), (far, 4))
    hold((near, 7), (near, 3))
    far[3] = flip(near[3], "gy", 2)
    far[7] = flip(near[7], "gy", 2)
    add((near, 5), (far, 5))
    add((near, 2), (far, 2), (near, 6), (far, 6))
    add((near, 3), (far, 3), (near, 7), (far, 7))
    meshes = [meshes[kind] for kind in range(4)]
    scalars = []
    for kind in range(4):
        slab_x, slab_z = x ^ (kind & 1), (z ^ (kind >> 1)) & 1
        real, imag = turns(kx_first * slab_x + 2 * kx_low * slab_z, 8)
        scalars.append(jnp.stack([real, imag]) * (1.0 / math.sqrt(NX * NY)))
    scalars = jnp.stack(scalars, axis=1)

    phase = jnp.stack(phases(kx_first, 2, cells_x // 2, NX))
    phase = jnp.broadcast_to(phase[:, :, None], (2, cells_x, LANES))
    owns = [columns_transform(meshes, scalars, phase, held_x, i, 256) for i in range(3)]
    partners = [flip(own, "gy", 1) for own in owns]

    turn_real, turn_imag = turns(ky_first, 4)
    cosine, sine = phases(ky_first, 4, cells_y // 4, NY)
    with_turn = [cosine * turn_real - sine * turn_imag, cosine * turn_imag + sine * turn_real]
    own, other = jnp.stack([cosine, sine]), jnp.stack(with_turn)
    scalars = jnp.concatenate(
        [jnp.where(core == 0, own, other), jnp.where(core == 0, other, own)]
    )
    result = None
    for i in range(3):
        result = rows_transform(owns[i], partners[i], scalars, held_y, 256, i, 3, result)
    return result


def solution(mesh):
    few = mesh.shape["gx"] == 8 and mesh.shape["gy"] == 4
    return jax.shard_map(
        particle_shards if few else dense_shards,
        mesh=mesh,
        in_specs=(
            P("gy", "gx", None),
            P("gy", "gx", None),
            P(None, "gy", "gx", None),
            P("gy", "gx", None),
            P("gy", "gx", None),
            P(None, "gy", "gx", None),
            P("gy", "gx"),
        ),
        out_specs=P(None, None, None, "gy", "gx"),
        check_vma=False,
    )
```

profile of v0, /device:TPU:1, one launch (start us, length us, event | category | flops | bytes accessed | tf_op | source)
XLA Modules:
  0.0 241.0 jit_solution(6823993766698630177)
XLA Ops:
  2.9 4.3 %sort.55 = (s32[2048]{0:T(1024)S(1)}, f32[2048]{0:T(1024)S(1)}, f32[2048]{0:T(1024)S(1)}, f32[2048]{0:T(1024)S(1)}) sort(s32[2048]{0:T(1024)S(1)} %fusion.15, f32[2048]{0:T(1024)S(1)} %fusion.20, f32[2048]{0:T(1024)S(1)} %get-tuple-element.72, f32[2048]{0:T(1024)S(1)} %get-tuple-element.71), dimensions={0}, to_apply=%region_1.2 | sort | flops 22528 | bytes 65536 | tf_op jit(solution)/shard_map/sort | solution.py:497
  7.2 2.1 collective-permute-start
  10.1 2.4 %abs_reduce_fusion = f32[]{:T(128)} fusion(f32[3,1,1,32768]{3,2,1,0:T(1,128)} %param.11), kind=kLoop, calls=%fused_computation.3 | loop fusion | flops 196607 | bytes 393220 | tf_op jit(solution)/shard_map/reduce_max | solution.py:512
  16.1 16.5 %sort.54 = (s32[32768]{0:T(1024)S(1)}, f32[32768]{0:T(1024)S(1)}, f32[32768]{0:T(1024)S(1)}, f32[32768]{0:T(1024)S(1)}) sort(s32[32768]{0:T(1024)S(1)} %fusion.4, f32[32768]{0:T(1024)S(1)} %bitcast.49, f32[32768]{0:T(1024)S(1)} %bitcast.48, f32[32768]{0:T(1024)S(1)} %bitcast.47), dimensions={0}, to_apply=%region_0.1 | sort | flops 491520 | bytes 1048576 | tf_op jit(solution)/shard_map/sort | solution.py:506
  32.6 2.0 convert_reduce_fusion
  38.9 2.3 collective-permute-start.3
  42.5 9.8 %deposit.7.refs_1_.refs_2_ = f32[3,512,1024]{2,1,0:T(8,128)S(1)} custom-call(f32[1]{0:T(128)} %bitcast.35.signs_ref, f32[4,34944]{1,0:T(4,128)S(1)} %maximum_maximum_fusion.refs_0_), custom_call_target="tpu_custom_call" | custom-call | flops 6870269952 | bytes 6291456 | tf_op jit(solution)/shard_map/deposit/pallas_call | solution.py:311
  55.1 10.3 %deposit.8.refs_2_ = f32[3,512,1024]{2,1,0:T(8,128)S(1)} custom-call(f32[1]{0:T(128)} %bitcast.10.signs_ref, f32[4,34944]{1,0:T(4,128)S(1)} %collective-permute-done.1.refs_0_, f32[3,512,1024]{2,1,0:T(8,128)S(1)} %deposit.7.refs_1_.refs_2_, f32[3,512,1024]{2,1,0:T(8,128)S(1)} %deposit.7.refs_1_.refs_2_), custom_call_target="tpu_custom_call" | custom-call | flops 6870269952 | bytes 6291456 | tf_op jit(solution)/shard_map/deposit/pallas_call | solution.py:311
  68.6 16.5 %deposit.9.refs_3_.refs_2_ = f32[3,512,1024]{2,1,0:T(8,128)S(1)} custom-call(f32[2]{0:T(128)S(1)} %pad_maximum_fusion.7.signs_ref, f32[4,34944]{1,0:T(4,128)S(1)} %collective-permute-done.2.refs_0_, f32[4,34944]{1,0:T(4,128)S(1)} %collective-permute-done.5.refs_1_, f32[3,512,1024]{2,1,0:T(8,128)S(1)} %deposit.8.refs_2_), custom_call_target="tpu_custom_call" | custom-call | flops 13740539904 | bytes 6291456 | tf_op jit(solution)/shard_map/deposit/pallas_call | solution.py:311
  85.2 3.7 %collective-permute-done.7.refs_0_ = f32[4,34944]{1,0:T(4,128)S(1)} collective-permute-done((f32[4,34944]{1,0:T(4,128)S(1)}, f32[4,34944]{1,0:T(4,128)S(1)}, u32[]{:S(2)}, u32[]{:S(2)}) %collective-permute-start.7) | collective-permute-done | bytes 559136 | tf_op jit(solution)/shard_map/ppermute | solution.py:39
  89.7 2.2 collective-permute-start.13
  93.3 17.3 %deposit.10.refs_3_.refs_0_ = f32[3,512,1024]{2,1,0:T(8,128)S(1)} custom-call(f32[2]{0:T(128)S(1)} %pad_maximum_fusion.6.signs_ref, f32[4,34944]{1,0:T(4,128)S(1)} %collective-permute-done.3.refs_0_, f32[4,34944]{1,0:T(4,128)S(1)} %collective-permute-done.6.refs_1_, f32[3,512,1024]{2,1,0:T(8,128)S(1)} %deposit.8.refs_2_, ...), custom_call_target="tpu_custom_call" | custom-call | flops 13740539904 | bytes 6291456 | tf_op jit(solution)/shard_map/deposit/pallas_call | solution.py:311
  112.2 3.2 %collective-permute-done.12.refs_1_ = f32[4,34944]{1,0:T(4,128)S(1)} collective-permute-done((f32[4,34944]{1,0:T(4,128)S(1)}, f32[4,34944]{1,0:T(4,128)S(1)}, u32[]{:S(2)}, u32[]{:S(2)}) %collective-permute-start.12) | collective-permute-done | bytes 559136 | tf_op jit(solution)/shard_map/ppermute | solution.py:39
  115.4 17.1 %deposit.11.refs_4_.refs_1_ = f32[3,512,1024]{2,1,0:T(8,128)S(1)} custom-call(f32[2]{0:T(128)S(1)} %pad_maximum_fusion.6.signs_ref, f32[4,34944]{1,0:T(4,128)S(1)} %collective-permute-done.7.refs_0_, f32[4,34944]{1,0:T(4,128)S(1)} %collective-permute-done.12.refs_1_, f32[3,512,1024]{2,1,0:T(8,128)S(1)} %deposit.9.refs_3_.refs_2_, ...), custom_call_target="tpu_custom_call" | custom-call | flops 13740539904 | bytes 6291456 | tf_op jit(solution)/shard_map/deposit/pallas_call | solution.py:311
  132.5 28.1 %deposit.12.refs_4_.refs_2_ = f32[3,512,1024]{2,1,0:T(8,128)S(1)} custom-call(f32[4]{0:T(128)S(1)} %pad_maximum_fusion.8.signs_ref, f32[4,34944]{1,0:T(4,128)S(1)} %collective-permute-done.4.refs_0_, f32[4,34944]{1,0:T(4,128)S(1)} %collective-permute-done.10.refs_1_, f32[4,34944]{1,0:T(4,128)S(1)} %collective-permute-done.8.refs_2_, ...), custom_call_target="tpu_custom_call" | custom-call | flops 27481079808 | bytes 6291456 | tf_op jit(solution)/shard_map/deposit/pallas_call | solution.py:311
  160.7 28.3 %deposit.13.refs_3_ = f32[3,512,1024]{2,1,0:T(8,128)S(1)} custom-call(f32[4]{0:T(128)S(1)} %pad_maximum_fusion.8.signs_ref, f32[4,34944]{1,0:T(4,128)S(1)} %collective-permute-done.9.refs_0_, f32[4,34944]{1,0:T(4,128)S(1)} %collective-permute-done.14.refs_1_, f32[4,34944]{1,0:T(4,128)S(1)} %collective-permute-done.11.refs_2_, ...), custom_call_target="tpu_custom_call" | custom-call | flops 27481079808 | bytes 6291456 | tf_op jit(solution)/shard_map/deposit/pallas_call | solution.py:311
  189.2 7.1 %columns_transform.5.own_ref = f32[2,1,512,1024]{3,2,1,0:T(8,128)} custom-call(f32[2,4]{1,0:T(2,128)S(1)} %pad_maximum_fusion.5.scalars_ref, f32[2,512,128]{2,1,0:T(8,128)S(1)} %broadcast_in_dim.17.phase_ref, bf16[2,512,1536]{2,1,0:T(8,128)(2,1)S(1)} %copy-done.1, f32[3,512,1024]{2,1,0:T(8,128)S(1)} %deposit.10.refs_3_.refs_0_, ...), custom_call_target="tpu_custom_call" | custom-call | flops 3221225472 | bytes 12582912 | tf_op jit(solution)/shard_map/columns_transform/pallas_call | solution.py:391
  196.3 3.5 %collective-permute-start.18 = (f32[2,1,512,1024]{3,2,1,0:T(8,128)}, f32[2,1,512,1024]{3,2,1,0:T(8,128)}, u32[]{:S(2)}, u32[]{:S(2)}) collective-permute-start(f32[2,1,512,1024]{3,2,1,0:T(8,128)} %columns_transform.5.own_ref), channel_id=1, source_target_pairs={{0,1},{1,0},{2,3},{3,2},{4,5},{5,4},{6,7},{7,6},{8,9},{9,8},{10,11... | collective-permute-start | bytes 12582920 | tf_op jit(solution)/shard_map/ppermute | solution.py:39
  199.8 7.1 %columns_transform.4.own_ref = f32[2,1,512,1024]{3,2,1,0:T(8,128)} custom-call(f32[2,4]{1,0:T(2,128)S(1)} %pad_maximum_fusion.5.scalars_ref, f32[2,512,128]{2,1,0:T(8,128)S(1)} %broadcast_in_dim.17.phase_ref, bf16[2,512,1536]{2,1,0:T(8,128)(2,1)S(1)} %copy-done.1, f32[3,512,1024]{2,1,0:T(8,128)S(1)} %deposit.10.refs_3_.refs_0_, ...), custom_call_target="tpu_custom_call" | custom-call | flops 3221225472 | bytes 12582912 | tf_op jit(solution)/shard_map/columns_transform/pallas_call | solution.py:391
  206.9 7.1 %columns_transform.3.own_ref = f32[2,1,512,1024]{3,2,1,0:T(8,128)} custom-call(f32[2,4]{1,0:T(2,128)S(1)} %pad_maximum_fusion.5.scalars_ref, f32[2,512,128]{2,1,0:T(8,128)S(1)} %broadcast_in_dim.17.phase_ref, bf16[2,512,1536]{2,1,0:T(8,128)(2,1)S(1)} %copy-done.1, f32[3,512,1024]{2,1,0:T(8,128)S(1)} %deposit.10.refs_3_.refs_0_, ...), custom_call_target="tpu_custom_call" | custom-call | flops 3221225472 | bytes 12582912 | tf_op jit(solution)/shard_map/columns_transform/pallas_call | solution.py:391
  215.1 2.8 %copy-done = bf16[4,512,1536]{2,1,0:T(8,128)(2,1)S(1)} copy-done((bf16[4,512,1536]{2,1,0:T(8,128)(2,1)S(1)}, bf16[4,512,1536]{2,1,0:T(8,128)(2,1)}, u32[]{:S(2)}) %copy-start) | copy-done | bytes 6291480
  217.9 7.8 %rows_transform.3.refs_0_ = f32[2,3,1,1024,512]{4,3,2,1,0:T(8,128)} custom-call(f32[4,1024]{1,0:T(4,128)S(1)} %pad_maximum_fusion.1.scalars_ref, bf16[4,512,1536]{2,1,0:T(8,128)(2,1)S(1)} %copy-done, f32[2,1,512,1024]{3,2,1,0:T(8,128)} %columns_transform.5.own_ref, f32[2,1,512,1024]{3,2,1,0:T(8,128)} %collective-permute-done.18.partner_ref), custom_call_target="tpu_custom_call" | custom-call | flops 3221225472 | bytes 12582912 | tf_op jit(solution)/shard_map/rows_transform/pallas_call | solution.py:449
  225.6 7.6 %rows_transform.4.refs_0_ = f32[2,3,1,1024,512]{4,3,2,1,0:T(8,128)} custom-call(f32[4,1024]{1,0:T(4,128)S(1)} %pad_maximum_fusion.1.scalars_ref, bf16[4,512,1536]{2,1,0:T(8,128)(2,1)S(1)} %copy-done, f32[2,1,512,1024]{3,2,1,0:T(8,128)} %columns_transform.4.own_ref, ...), custom_call_target="tpu_custom_call", output_to_operand_aliasing={{}: (4, {})} | custom-call | flops 3221225472 | bytes 12582912 | tf_op jit(solution)/shard_map/rows_transform/pallas_call | solution.py:449
  233.2 7.6 %rows_transform.5 = f32[2,3,1,1024,512]{4,3,2,1,0:T(8,128)} custom-call(f32[4,1024]{1,0:T(4,128)S(1)} %pad_maximum_fusion.1.scalars_ref, bf16[4,512,1536]{2,1,0:T(8,128)(2,1)S(1)} %copy-done, f32[2,1,512,1024]{3,2,1,0:T(8,128)} %columns_transform.3.own_ref, f32[2,1,512,1024]{3,2,1,0:T(8,128)} %collective-permute-done.16.partner_ref, ...), custom_call_target="tpu_custom_call", output_to_operand_aliasing={{}: (4, {})} | custom-call | flops 3221225472 | bytes 12582912 | tf_op jit(solution)/shard_map/rows_transform/pallas_call | solution.py:449
  (69 shorter events, 20.9 us)
Async XLA Ops:
  7.2 27.6 %collective-permute-start = (f32[4,2048]{1,0:T(4,128)S(1)}, f32[4,2048]{1,0:T(4,128)S(1)}, u32[]{:S(2)}, u32[]{:S(2)}) collective-permute-start(f32[4,2048]{1,0:T(4,128)S(1)} %pad_maximum_fusion), channel_id=1, source_target_pairs={{0,4},{4,8},{8,12},{12,16},{16,20},{20,24},{24,28},{28,0},{1,5},{5... | collective-permute-start | bytes 98312 | tf_op jit(solution)/shard_map/ppermute | solution.py:34
  37.6 27.9 %collective-permute-start.4 = (f32[4,34944]{1,0:T(4,128)S(1)}, f32[4,34944]{1,0:T(4,128)S(1)}, u32[]{:S(2)}, u32[]{:S(2)}) collective-permute-start(f32[4,34944]{1,0:T(4,128)S(1)} %maximum_maximum_fusion.refs_0_), channel_id=1, source_target_pairs={{0,8},{4,12},{8,0},{12,4},{16,24},{20,28},{24,16},{28,20},{1,9},{5... | collective-permute-start | bytes 1677320 | tf_op jit(solution)/shard_map/ppermute | solution.py:39
  38.9 26.5 %collective-permute-start.3 = (f32[4,34944]{1,0:T(4,128)S(1)}, f32[4,34944]{1,0:T(4,128)S(1)}, u32[]{:S(2)}, u32[]{:S(2)}) collective-permute-start(f32[4,34944]{1,0:T(4,128)S(1)} %maximum_maximum_fusion.refs_0_), channel_id=1, source_target_pairs={{0,16},{4,20},{8,24},{12,28},{16,0},{20,4},{24,8},{28,12},{1,17},{... | collective-permute-start | bytes 1677320 | tf_op jit(solution)/shard_map/ppermute | solution.py:39
  41.2 12.6 %collective-permute-start.2 = (f32[4,34944]{1,0:T(4,128)S(1)}, f32[4,34944]{1,0:T(4,128)S(1)}, u32[]{:S(2)}, u32[]{:S(2)}) collective-permute-start(f32[4,34944]{1,0:T(4,128)S(1)} %maximum_maximum_fusion.refs_0_), channel_id=1, source_target_pairs={{0,4},{4,0},{8,12},{12,8},{16,20},{20,16},{24,28},{28,24},{1,5},{5... | collective-permute-start | bytes 1677320 | tf_op jit(solution)/shard_map/ppermute | solution.py:39
  41.3 13.8 %collective-permute-start.1 = (f32[4,34944]{1,0:T(4,128)S(1)}, f32[4,34944]{1,0:T(4,128)S(1)}, u32[]{:S(2)}, u32[]{:S(2)}) collective-permute-start(f32[4,34944]{1,0:T(4,128)S(1)} %maximum_maximum_fusion.refs_0_), channel_id=1, source_target_pairs={{0,2},{1,3},{2,0},{3,1},{4,6},{5,7},{6,4},{7,5},{8,10},{9,11},{10,... | collective-permute-start | bytes 1677320 | tf_op jit(solution)/shard_map/ppermute | solution.py:39
  53.9 14.3 %collective-permute-start.5 = (f32[4,34944]{1,0:T(4,128)S(1)}, f32[4,34944]{1,0:T(4,128)S(1)}, u32[]{:S(2)}, u32[]{:S(2)}) collective-permute-start(f32[4,34944]{1,0:T(4,128)S(1)} %collective-permute-done.2.refs_0_), channel_id=1, source_target_pairs={{0,2},{1,3},{2,0},{3,1},{4,6},{5,7},{6,4},{7,5},{8,10},{9,11},{10,... | collective-permute-start | bytes 1677320 | tf_op jit(solution)/shard_map/ppermute | solution.py:39
  65.5 19.7 %collective-permute-start.10 = (f32[4,34944]{1,0:T(4,128)S(1)}, f32[4,34944]{1,0:T(4,128)S(1)}, u32[]{:S(2)}, u32[]{:S(2)}) collective-permute-start(f32[4,34944]{1,0:T(4,128)S(1)} %collective-permute-done.4.refs_0_), channel_id=1, source_target_pairs={{0,2},{1,3},{2,0},{3,1},{4,6},{5,7},{6,4},{7,5},{8,10},{9,11},{10,... | collective-permute-start | bytes 1677320 | tf_op jit(solution)/shard_map/ppermute | solution.py:39
  65.8 19.4 %collective-permute-start.9 = (f32[4,34944]{1,0:T(4,128)S(1)}, f32[4,34944]{1,0:T(4,128)S(1)}, u32[]{:S(2)}, u32[]{:S(2)}) collective-permute-start(f32[4,34944]{1,0:T(4,128)S(1)} %collective-permute-done.4.refs_0_), channel_id=1, source_target_pairs={{0,4},{4,0},{8,12},{12,8},{16,20},{20,16},{24,28},{28,24},{1,5},{5... | collective-permute-start | bytes 1677320 | tf_op jit(solution)/shard_map/ppermute | solution.py:39
  66.7 18.5 %collective-permute-start.8 = (f32[4,34944]{1,0:T(4,128)S(1)}, f32[4,34944]{1,0:T(4,128)S(1)}, u32[]{:S(2)}, u32[]{:S(2)}) collective-permute-start(f32[4,34944]{1,0:T(4,128)S(1)} %collective-permute-done.3.refs_0_), channel_id=1, source_target_pairs={{0,8},{4,12},{8,0},{12,4},{16,24},{20,28},{24,16},{28,20},{1,9},{5... | collective-permute-start | bytes 1677320 | tf_op jit(solution)/shard_map/ppermute | solution.py:39
  67.7 21.2 %collective-permute-start.7 = (f32[4,34944]{1,0:T(4,128)S(1)}, f32[4,34944]{1,0:T(4,128)S(1)}, u32[]{:S(2)}, u32[]{:S(2)}) collective-permute-start(f32[4,34944]{1,0:T(4,128)S(1)} %collective-permute-done.3.refs_0_), channel_id=1, source_target_pairs={{0,4},{4,0},{8,12},{12,8},{16,20},{20,16},{24,28},{28,24},{1,5},{5... | collective-permute-start | bytes 1677320 | tf_op jit(solution)/shard_map/ppermute | solution.py:39
  68.1 21.5 %collective-permute-start.6 = (f32[4,34944]{1,0:T(4,128)S(1)}, f32[4,34944]{1,0:T(4,128)S(1)}, u32[]{:S(2)}, u32[]{:S(2)}) collective-permute-start(f32[4,34944]{1,0:T(4,128)S(1)} %collective-permute-done.3.refs_0_), channel_id=1, source_target_pairs={{0,2},{1,3},{2,0},{3,1},{4,6},{5,7},{6,4},{7,5},{8,10},{9,11},{10,... | collective-permute-start | bytes 1677320 | tf_op jit(solution)/shard_map/ppermute | solution.py:39
  89.7 42.9 %collective-permute-start.13 = (f32[4,34944]{1,0:T(4,128)S(1)}, f32[4,34944]{1,0:T(4,128)S(1)}, u32[]{:S(2)}, u32[]{:S(2)}) collective-permute-start(f32[4,34944]{1,0:T(4,128)S(1)} %collective-permute-done.8.refs_2_), channel_id=1, source_target_pairs={{0,2},{1,3},{2,0},{3,1},{4,6},{5,7},{6,4},{7,5},{8,10},{9,11},{10,... | collective-permute-start | bytes 1677320 | tf_op jit(solution)/shard_map/ppermute | solution.py:39
  91.9 18.8 %collective-permute-start.11 = (f32[4,34944]{1,0:T(4,128)S(1)}, f32[4,34944]{1,0:T(4,128)S(1)}, u32[]{:S(2)}, u32[]{:S(2)}) collective-permute-start(f32[4,34944]{1,0:T(4,128)S(1)} %collective-permute-done.8.refs_2_), channel_id=1, source_target_pairs={{0,4},{4,0},{8,12},{12,8},{16,20},{20,16},{24,28},{28,24},{1,5},{5... | collective-permute-start | bytes 1677320 | tf_op jit(solution)/shard_map/ppermute | solution.py:39
  92.0 23.5 %collective-permute-start.12 = (f32[4,34944]{1,0:T(4,128)S(1)}, f32[4,34944]{1,0:T(4,128)S(1)}, u32[]{:S(2)}, u32[]{:S(2)}) collective-permute-start(f32[4,34944]{1,0:T(4,128)S(1)} %collective-permute-done.6.refs_1_), channel_id=1, source_target_pairs={{0,4},{4,0},{8,12},{12,8},{16,20},{20,16},{24,28},{28,24},{1,5},{5... | collective-permute-start | bytes 1677320 | tf_op jit(solution)/shard_map/ppermute | solution.py:39
  110.7 50.0 %collective-permute-start.14 = (f32[4,34944]{1,0:T(4,128)S(1)}, f32[4,34944]{1,0:T(4,128)S(1)}, u32[]{:S(2)}, u32[]{:S(2)}) collective-permute-start(f32[4,34944]{1,0:T(4,128)S(1)} %collective-permute-done.9.refs_0_), channel_id=1, source_target_pairs={{0,2},{1,3},{2,0},{3,1},{4,6},{5,7},{6,4},{7,5},{8,10},{9,11},{10,... | collective-permute-start | bytes 1677320 | tf_op jit(solution)/shard_map/ppermute | solution.py:39
  110.7 49.9 %collective-permute-start.15 = (f32[4,34944]{1,0:T(4,128)S(1)}, f32[4,34944]{1,0:T(4,128)S(1)}, u32[]{:S(2)}, u32[]{:S(2)}) collective-permute-start(f32[4,34944]{1,0:T(4,128)S(1)} %collective-permute-done.11.refs_2_), channel_id=1, source_target_pairs={{0,2},{1,3},{2,0},{3,1},{4,6},{5,7},{6,4},{7,5},{8,10},{9,11},{10,... | collective-permute-start | bytes 1677320 | tf_op jit(solution)/shard_map/ppermute | solution.py:39
  160.7 28.5 %copy-start.1 = (bf16[2,512,1536]{2,1,0:T(8,128)(2,1)S(1)}, bf16[2,512,1536]{2,1,0:T(8,128)(2,1)}, u32[]{:S(2)}) copy-start(bf16[2,512,1536]{2,1,0:T(8,128)(2,1)} %constant.207.clone.held_ref) | copy-start | bytes 9437188
  196.3 18.7 %collective-permute-start.18 = (f32[2,1,512,1024]{3,2,1,0:T(8,128)}, f32[2,1,512,1024]{3,2,1,0:T(8,128)}, u32[]{:S(2)}, u32[]{:S(2)}) collective-permute-start(f32[2,1,512,1024]{3,2,1,0:T(8,128)} %columns_transform.5.own_ref), channel_id=1, source_target_pairs={{0,1},{1,0},{2,3},{3,2},{4,5},{5,4},{6,7},{7,6},{8,9},{9,8},{10,11... | collective-permute-start | bytes 12582920 | tf_op jit(solution)/shard_map/ppermute | solution.py:39
  206.9 18.7 %collective-permute-start.17 = (f32[2,1,512,1024]{3,2,1,0:T(8,128)}, f32[2,1,512,1024]{3,2,1,0:T(8,128)}, u32[]{:S(2)}, u32[]{:S(2)}) collective-permute-start(f32[2,1,512,1024]{3,2,1,0:T(8,128)} %columns_transform.4.own_ref), channel_id=1, source_target_pairs={{0,1},{1,0},{2,3},{3,2},{4,5},{5,4},{6,7},{7,6},{8,9},{9,8},{10,11... | collective-permute-start | bytes 12582920 | tf_op jit(solution)/shard_map/ppermute | solution.py:39
  214.0 19.2 %collective-permute-start.16 = (f32[2,1,512,1024]{3,2,1,0:T(8,128)}, f32[2,1,512,1024]{3,2,1,0:T(8,128)}, u32[]{:S(2)}, u32[]{:S(2)}) collective-permute-start(f32[2,1,512,1024]{3,2,1,0:T(8,128)} %columns_transform.3.own_ref), channel_id=1, source_target_pairs={{0,1},{1,0},{2,3},{3,2},{4,5},{5,4},{6,7},{7,6},{8,9},{9,8},{10,11... | collective-permute-start | bytes 12582920 | tf_op jit(solution)/shard_map/ppermute | solution.py:39
  215.1 2.8 %copy-start = (bf16[4,512,1536]{2,1,0:T(8,128)(2,1)S(1)}, bf16[4,512,1536]{2,1,0:T(8,128)(2,1)}, u32[]{:S(2)}) copy-start(bf16[4,512,1536]{2,1,0:T(8,128)(2,1)} %constant.208.clone.held_ref) | copy-start | bytes 18874372
where the time goes:
time: 244 us; the launch traced here: 241 us
  Pallas kernels  172 us (70%)
  other arithmetic  31.2 us (13%)
  starting transfers between devices  20.7 us (8%)
  waiting for transfers between devices  9.27 us (4%)
  local copies, waits for them, and re-layouts  4.78 us (2%)
  between operations  3.37 us (1%)
    pallas_call x7, Pallas kernels, deposit(): pl.pallas_call(kernel, grid=(cells_x // (GROUP * BIN_COLS),), in_specs=[p...  127 us
    pallas_call x3, Pallas kernels, rows_transform(): pl.pallas_call(kernel, grid=(cells_x // block,), in_specs=[pl.BlockSpec(m...  23 us
    pallas_call x3, Pallas kernels, columns_transform(): pl.pallas_call(kernel, grid=(cells_y // block,), in_specs=[pl.BlockSpec(m...  21.3 us
    ppermute x18, starting transfers between devices, flip(): lax.ppermute(value, axis, [(source, source ^ mask) for source in range(co...  18.6 us
    sort x1, other arithmetic, particle_shards(): lax.sort((key, *(resident_strength[i].reshape(-1) for i in range(3))), nu...  16.5 us
    ppermute x18, waiting for transfers between devices, flip(): lax.ppermute(value, axis, [(source, source ^ mask) for source in range(co...  9.27 us
  transfers between devices with their start and end apart: 19, of which 4 were waited for; matrix products, arithmetic and copies ran while one was open for 10% of the time, Pallas kernels for 53%

commit v1 on v0

--- a/solution.py
+++ b/solution.py
@@ -399,7 +399,7 @@
         + [pl.BlockSpec(memory_space=pltpu.VMEM)] * count,
         out_specs=pl.BlockSpec((2, 1, cells_x, block), lambda g: (0, 0, 0, g)),
         out_shape=jax.ShapeDtypeStruct((2, 1, cells_x, cells_y), jnp.float32),
-        compiler_params=pltpu.CompilerParams(vmem_limit_bytes=14 << 20),
+        compiler_params=pltpu.CompilerParams(vmem_limit_bytes=12 << 20),
         cost_estimate=pl.CostEstimate(
             flops=12 * cells_x * cells_x * cells_y,
             bytes_accessed=(count + 2) * 4 * cells_x * cells_y,
@@ -570,17 +570,18 @@
     near[5] = flip(near[4], "gx", 1)
     near[6] = flip(near[4], "gx", 2)
     far[2] = flip(near[2], "gy", 2)
-    near[3] = flip(near[2], "gx", 1)
+    near[3] = flip(near[1], "gx", 2)
     add((near, 1), (far, 1))
-    hold((far, 4), (near, 5), (near, 6), (near, 3), (far, 2))
+    hold((far, 4), (near, 6))
     far[5] = flip(far[4], "gx", 1)
     far[6] = flip(near[6], "gy", 2)
+    add((near, 4), (far, 4))
+    hold((near, 6), (near, 3))
     near[7] = flip(near[6], "gx", 1)
-    add((near, 4), (far, 4))
-    hold((near, 7), (near, 3))
     far[3] = flip(near[3], "gy", 2)
+    add((near, 5), (far, 5))
+    hold((near, 7))
     far[7] = flip(near[7], "gy", 2)
-    add((near, 5), (far, 5))
     add((near, 2), (far, 2), (near, 6), (far, 6))
     add((near, 3), (far, 3), (near, 7), (far, 7))
     meshes = [meshes[kind] for kind in range(4)]
@@ -593,7 +594,7 @@
 
     phase = jnp.stack(phases(kx_first, 2, cells_x // 2, NX))
     phase = jnp.broadcast_to(phase[:, :, None], (2, cells_x, LANES))
-    owns = [columns_transform(meshes, scalars, phase, held_x, i, 256) for i in range(3)]
+    owns = [columns_transform(meshes, scalars, phase, held_x, i, 512) for i in range(3)]
     partners = [flip(own, "gy", 1) for own in owns]
 
     turn_real, turn_imag = turns(ky_first, 4)

time: 244 us -> 236 us (0.967)
  waiting for transfers between devices: 9.27 us -> 1.57 us
    ppermute x18, waiting for transfers between devices: 9.27 us -> 1.57 us  [flip(): lax.ppermute(value, axis, [(source, source ^ mask) for source in range(co...]
  transfers between devices with their start and end apart: 19 -> 19, of which waited for: 4 -> 1; matrix products, arithmetic and copies ran while one was open for 10% -> 11% of each run, Pallas kernels for 53% -> 55%
where the time goes in v1:
time: 236 us; the launch traced here: 233 us
  Pallas kernels  170 us (72%)
  other arithmetic  31.2 us (13%)
  starting transfers between devices  22.2 us (9%)
  local copies, waits for them, and re-layouts  4.78 us (2%)
  between operations  3.36 us (1%)
    pallas_call x7, Pallas kernels, deposit(): pl.pallas_call(kernel, grid=(cells_x // (GROUP * BIN_COLS),), in_specs=[p...  127 us
    pallas_call x3, Pallas kernels, rows_transform(): pl.pallas_call(kernel, grid=(cells_x // block,), in_specs=[pl.BlockSpec(m...  22.8 us
    ppermute x18, starting transfers between devices, flip(): lax.ppermute(value, axis, [(source, source ^ mask) for source in range(co...  20.1 us
    pallas_call x3, Pallas kernels, columns_transform(): pl.pallas_call(kernel, grid=(cells_y // block,), in_specs=[pl.BlockSpec(m...  19.8 us
    sort x1, other arithmetic, particle_shards(): lax.sort((key, *(resident_strength[i].reshape(-1) for i in range(3))), nu...  16.5 us
  transfers between devices with their start and end apart: 19, of which 1 were waited for; matrix products, arithmetic and copies ran while one was open for 11% of the time, Pallas kernels for 55%

profile of v1, /device:TPU:1, one launch (start us, length us, event | category | flops | bytes accessed | tf_op | source)
XLA Modules:
  0.0 233.1 jit_solution(3338293203322605086)
XLA Ops:
  2.9 4.3 %sort.55 = (s32[2048]{0:T(1024)S(1)}, f32[2048]{0:T(1024)S(1)}, f32[2048]{0:T(1024)S(1)}, f32[2048]{0:T(1024)S(1)}) sort(s32[2048]{0:T(1024)S(1)} %fusion.15, f32[2048]{0:T(1024)S(1)} %fusion.20, f32[2048]{0:T(1024)S(1)} %get-tuple-element.70, f32[2048]{0:T(1024)S(1)} %get-tuple-element.69), dimensions={0}, to_apply=%region_1.2 | sort | flops 22528 | bytes 65536 | tf_op jit(solution)/shard_map/sort | solution.py:497
  7.2 2.1 collective-permute-start
  10.1 2.4 %abs_reduce_fusion = f32[]{:T(128)} fusion(f32[3,1,1,32768]{3,2,1,0:T(1,128)} %param.11), kind=kLoop, calls=%fused_computation.3 | loop fusion | flops 196607 | bytes 393220 | tf_op jit(solution)/shard_map/reduce_max | solution.py:512
  16.1 16.5 %sort.54 = (s32[32768]{0:T(1024)S(1)}, f32[32768]{0:T(1024)S(1)}, f32[32768]{0:T(1024)S(1)}, f32[32768]{0:T(1024)S(1)}) sort(s32[32768]{0:T(1024)S(1)} %fusion.4, f32[32768]{0:T(1024)S(1)} %bitcast.49, f32[32768]{0:T(1024)S(1)} %bitcast.48, f32[32768]{0:T(1024)S(1)} %bitcast.47), dimensions={0}, to_apply=%region_0.1 | sort | flops 491520 | bytes 1048576 | tf_op jit(solution)/shard_map/sort | solution.py:506
  32.6 2.0 convert_reduce_fusion
  37.6 1.4 collective-permute-start.4
  38.9 2.3 collective-permute-start.3
  42.5 9.8 %deposit.7.refs_1_.refs_2_ = f32[3,512,1024]{2,1,0:T(8,128)S(1)} custom-call(f32[1]{0:T(128)} %bitcast.35.signs_ref, f32[4,34944]{1,0:T(4,128)S(1)} %maximum_maximum_fusion.refs_0_), custom_call_target="tpu_custom_call" | custom-call | flops 6870269952 | bytes 6291456 | tf_op jit(solution)/shard_map/deposit/pallas_call | solution.py:311
  52.4 1.5 collective-permute-done.2.refs_0_
  55.1 10.3 %deposit.8.refs_2_ = f32[3,512,1024]{2,1,0:T(8,128)S(1)} custom-call(f32[1]{0:T(128)} %bitcast.10.signs_ref, f32[4,34944]{1,0:T(4,128)S(1)} %collective-permute-done.1.refs_0_, f32[3,512,1024]{2,1,0:T(8,128)S(1)} %deposit.7.refs_1_.refs_2_, f32[3,512,1024]{2,1,0:T(8,128)S(1)} %deposit.7.refs_1_.refs_2_), custom_call_target="tpu_custom_call" | custom-call | flops 6870269952 | bytes 6291456 | tf_op jit(solution)/shard_map/deposit/pallas_call | solution.py:311
  68.6 16.5 %deposit.9.refs_3_.refs_2_ = f32[3,512,1024]{2,1,0:T(8,128)S(1)} custom-call(f32[2]{0:T(128)S(1)} %pad_maximum_fusion.7.signs_ref, f32[4,34944]{1,0:T(4,128)S(1)} %collective-permute-done.2.refs_0_, f32[4,34944]{1,0:T(4,128)S(1)} %collective-permute-done.5.refs_1_, f32[3,512,1024]{2,1,0:T(8,128)S(1)} %deposit.8.refs_2_), custom_call_target="tpu_custom_call" | custom-call | flops 13740539904 | bytes 6291456 | tf_op jit(solution)/shard_map/deposit/pallas_call | solution.py:311
  85.2 1.3 collective-permute-start.10
  86.7 17.3 %deposit.10.refs_3_.refs_0_ = f32[3,512,1024]{2,1,0:T(8,128)S(1)} custom-call(f32[2]{0:T(128)S(1)} %pad_maximum_fusion.6.signs_ref, f32[4,34944]{1,0:T(4,128)S(1)} %collective-permute-done.3.refs_0_, f32[4,34944]{1,0:T(4,128)S(1)} %collective-permute-done.6.refs_1_, f32[3,512,1024]{2,1,0:T(8,128)S(1)} %deposit.8.refs_2_, ...), custom_call_target="tpu_custom_call" | custom-call | flops 13740539904 | bytes 6291456 | tf_op jit(solution)/shard_map/deposit/pallas_call | solution.py:311
  105.6 17.1 %deposit.11.refs_4_.refs_1_ = f32[3,512,1024]{2,1,0:T(8,128)S(1)} custom-call(f32[2]{0:T(128)S(1)} %pad_maximum_fusion.6.signs_ref, f32[4,34944]{1,0:T(4,128)S(1)} %collective-permute-done.9.refs_0_, f32[4,34944]{1,0:T(4,128)S(1)} %collective-permute-done.10.refs_1_, f32[3,512,1024]{2,1,0:T(8,128)S(1)} %deposit.9.refs_3_.refs_2_, ...), custom_call_target="tpu_custom_call" | custom-call | flops 13740539904 | bytes 6291456 | tf_op jit(solution)/shard_map/deposit/pallas_call | solution.py:311
  123.8 28.1 %deposit.12.refs_4_.refs_2_ = f32[3,512,1024]{2,1,0:T(8,128)S(1)} custom-call(f32[4]{0:T(128)S(1)} %pad_maximum_fusion.8.signs_ref, f32[4,34944]{1,0:T(4,128)S(1)} %collective-permute-done.4.refs_0_, f32[4,34944]{1,0:T(4,128)S(1)} %collective-permute-done.12.refs_1_, f32[4,34944]{1,0:T(4,128)S(1)} %collective-permute-done.7.refs_2_, ...), custom_call_target="tpu_custom_call" | custom-call | flops 27481079808 | bytes 6291456 | tf_op jit(solution)/shard_map/deposit/pallas_call | solution.py:311
  151.9 28.3 %deposit.13.refs_3_ = f32[3,512,1024]{2,1,0:T(8,128)S(1)} custom-call(f32[4]{0:T(128)S(1)} %pad_maximum_fusion.8.signs_ref, f32[4,34944]{1,0:T(4,128)S(1)} %collective-permute-done.8.refs_0_, f32[4,34944]{1,0:T(4,128)S(1)} %collective-permute-done.14.refs_1_, f32[4,34944]{1,0:T(4,128)S(1)} %collective-permute-done.11.refs_2_, ...), custom_call_target="tpu_custom_call" | custom-call | flops 27481079808 | bytes 6291456 | tf_op jit(solution)/shard_map/deposit/pallas_call | solution.py:311
  180.4 6.5 %columns_transform.5.own_ref = f32[2,1,512,1024]{3,2,1,0:T(8,128)} custom-call(f32[2,4]{1,0:T(2,128)S(1)} %pad_maximum_fusion.5.scalars_ref, f32[2,512,128]{2,1,0:T(8,128)S(1)} %broadcast_in_dim.17.phase_ref, bf16[2,512,1536]{2,1,0:T(8,128)(2,1)S(1)} %copy-done.1, f32[3,512,1024]{2,1,0:T(8,128)S(1)} %deposit.10.refs_3_.refs_0_, ...), custom_call_target="tpu_custom_call" | custom-call | flops 3221225472 | bytes 12582912 | tf_op jit(solution)/shard_map/columns_transform/pallas_call | solution.py:391
  186.9 6.0 %collective-permute-start.18 = (f32[2,1,512,1024]{3,2,1,0:T(8,128)}, f32[2,1,512,1024]{3,2,1,0:T(8,128)}, u32[]{:S(2)}, u32[]{:S(2)}) collective-permute-start(f32[2,1,512,1024]{3,2,1,0:T(8,128)} %columns_transform.5.own_ref), channel_id=1, source_target_pairs={{0,1},{1,0},{2,3},{3,2},{4,5},{5,4},{6,7},{7,6},{8,9},{9,8},{10,11... | collective-permute-start | bytes 12582920 | tf_op jit(solution)/shard_map/ppermute | solution.py:39
  193.0 6.6 %columns_transform.4.own_ref = f32[2,1,512,1024]{3,2,1,0:T(8,128)} custom-call(f32[2,4]{1,0:T(2,128)S(1)} %pad_maximum_fusion.5.scalars_ref, f32[2,512,128]{2,1,0:T(8,128)S(1)} %broadcast_in_dim.17.phase_ref, bf16[2,512,1536]{2,1,0:T(8,128)(2,1)S(1)} %copy-done.1, f32[3,512,1024]{2,1,0:T(8,128)S(1)} %deposit.10.refs_3_.refs_0_, ...), custom_call_target="tpu_custom_call" | custom-call | flops 3221225472 | bytes 12582912 | tf_op jit(solution)/shard_map/columns_transform/pallas_call | solution.py:391
  199.6 6.7 %columns_transform.3.own_ref = f32[2,1,512,1024]{3,2,1,0:T(8,128)} custom-call(f32[2,4]{1,0:T(2,128)S(1)} %pad_maximum_fusion.5.scalars_ref, f32[2,512,128]{2,1,0:T(8,128)S(1)} %broadcast_in_dim.17.phase_ref, bf16[2,512,1536]{2,1,0:T(8,128)(2,1)S(1)} %copy-done.1, f32[3,512,1024]{2,1,0:T(8,128)S(1)} %deposit.10.refs_3_.refs_0_, ...), custom_call_target="tpu_custom_call" | custom-call | flops 3221225472 | bytes 12582912 | tf_op jit(solution)/shard_map/columns_transform/pallas_call | solution.py:391
  207.3 2.8 %copy-done = bf16[4,512,1536]{2,1,0:T(8,128)(2,1)S(1)} copy-done((bf16[4,512,1536]{2,1,0:T(8,128)(2,1)S(1)}, bf16[4,512,1536]{2,1,0:T(8,128)(2,1)}, u32[]{:S(2)}) %copy-start) | copy-done | bytes 6291480
  210.1 7.6 %rows_transform.3.refs_0_ = f32[2,3,1,1024,512]{4,3,2,1,0:T(8,128)} custom-call(f32[4,1024]{1,0:T(4,128)S(1)} %pad_maximum_fusion.1.scalars_ref, bf16[4,512,1536]{2,1,0:T(8,128)(2,1)S(1)} %copy-done, f32[2,1,512,1024]{3,2,1,0:T(8,128)} %columns_transform.5.own_ref, f32[2,1,512,1024]{3,2,1,0:T(8,128)} %collective-permute-done.18.partner_ref), custom_call_target="tpu_custom_call" | custom-call | flops 3221225472 | bytes 12582912 | tf_op jit(solution)/shard_map/rows_transform/pallas_call | solution.py:449
  217.7 7.6 %rows_transform.4.refs_0_ = f32[2,3,1,1024,512]{4,3,2,1,0:T(8,128)} custom-call(f32[4,1024]{1,0:T(4,128)S(1)} %pad_maximum_fusion.1.scalars_ref, bf16[4,512,1536]{2,1,0:T(8,128)(2,1)S(1)} %copy-done, f32[2,1,512,1024]{3,2,1,0:T(8,128)} %columns_transform.4.own_ref, ...), custom_call_target="tpu_custom_call", output_to_operand_aliasing={{}: (4, {})} | custom-call | flops 3221225472 | bytes 12582912 | tf_op jit(solution)/shard_map/rows_transform/pallas_call | solution.py:449
  225.3 7.6 %rows_transform.5 = f32[2,3,1,1024,512]{4,3,2,1,0:T(8,128)} custom-call(f32[4,1024]{1,0:T(4,128)S(1)} %pad_maximum_fusion.1.scalars_ref, bf16[4,512,1536]{2,1,0:T(8,128)(2,1)S(1)} %copy-done, f32[2,1,512,1024]{3,2,1,0:T(8,128)} %columns_transform.3.own_ref, f32[2,1,512,1024]{3,2,1,0:T(8,128)} %collective-permute-done.16.partner_ref, ...), custom_call_target="tpu_custom_call", output_to_operand_aliasing={{}: (4, {})} | custom-call | flops 3221225472 | bytes 12582912 | tf_op jit(solution)/shard_map/rows_transform/pallas_call | solution.py:449
  (69 shorter events, 17.1 us)
Async XLA Ops:
  7.2 27.6 %collective-permute-start = (f32[4,2048]{1,0:T(4,128)S(1)}, f32[4,2048]{1,0:T(4,128)S(1)}, u32[]{:S(2)}, u32[]{:S(2)}) collective-permute-start(f32[4,2048]{1,0:T(4,128)S(1)} %pad_maximum_fusion), channel_id=1, source_target_pairs={{0,4},{4,8},{8,12},{12,16},{16,20},{20,24},{24,28},{28,0},{1,5},{5... | collective-permute-start | bytes 98312 | tf_op jit(solution)/shard_map/ppermute | solution.py:34
  37.6 27.9 %collective-permute-start.4 = (f32[4,34944]{1,0:T(4,128)S(1)}, f32[4,34944]{1,0:T(4,128)S(1)}, u32[]{:S(2)}, u32[]{:S(2)}) collective-permute-start(f32[4,34944]{1,0:T(4,128)S(1)} %maximum_maximum_fusion.refs_0_), channel_id=1, source_target_pairs={{0,8},{4,12},{8,0},{12,4},{16,24},{20,28},{24,16},{28,20},{1,9},{5... | collective-permute-start | bytes 1677320 | tf_op jit(solution)/shard_map/ppermute | solution.py:39
  38.9 26.5 %collective-permute-start.3 = (f32[4,34944]{1,0:T(4,128)S(1)}, f32[4,34944]{1,0:T(4,128)S(1)}, u32[]{:S(2)}, u32[]{:S(2)}) collective-permute-start(f32[4,34944]{1,0:T(4,128)S(1)} %maximum_maximum_fusion.refs_0_), channel_id=1, source_target_pairs={{0,16},{4,20},{8,24},{12,28},{16,0},{20,4},{24,8},{28,12},{1,17},{... | collective-permute-start | bytes 1677320 | tf_op jit(solution)/shard_map/ppermute | solution.py:39
  41.2 12.6 %collective-permute-start.2 = (f32[4,34944]{1,0:T(4,128)S(1)}, f32[4,34944]{1,0:T(4,128)S(1)}, u32[]{:S(2)}, u32[]{:S(2)}) collective-permute-start(f32[4,34944]{1,0:T(4,128)S(1)} %maximum_maximum_fusion.refs_0_), channel_id=1, source_target_pairs={{0,4},{4,0},{8,12},{12,8},{16,20},{20,16},{24,28},{28,24},{1,5},{5... | collective-permute-start | bytes 1677320 | tf_op jit(solution)/shard_map/ppermute | solution.py:39
  41.3 13.8 %collective-permute-start.1 = (f32[4,34944]{1,0:T(4,128)S(1)}, f32[4,34944]{1,0:T(4,128)S(1)}, u32[]{:S(2)}, u32[]{:S(2)}) collective-permute-start(f32[4,34944]{1,0:T(4,128)S(1)} %maximum_maximum_fusion.refs_0_), channel_id=1, source_target_pairs={{0,2},{1,3},{2,0},{3,1},{4,6},{5,7},{6,4},{7,5},{8,10},{9,11},{10,... | collective-permute-start | bytes 1677320 | tf_op jit(solution)/shard_map/ppermute | solution.py:39
  53.9 14.3 %collective-permute-start.5 = (f32[4,34944]{1,0:T(4,128)S(1)}, f32[4,34944]{1,0:T(4,128)S(1)}, u32[]{:S(2)}, u32[]{:S(2)}) collective-permute-start(f32[4,34944]{1,0:T(4,128)S(1)} %collective-permute-done.2.refs_0_), channel_id=1, source_target_pairs={{0,2},{1,3},{2,0},{3,1},{4,6},{5,7},{6,4},{7,5},{8,10},{9,11},{10,... | collective-permute-start | bytes 1677320 | tf_op jit(solution)/shard_map/ppermute | solution.py:39
  65.5 39.7 %collective-permute-start.9 = (f32[4,34944]{1,0:T(4,128)S(1)}, f32[4,34944]{1,0:T(4,128)S(1)}, u32[]{:S(2)}, u32[]{:S(2)}) collective-permute-start(f32[4,34944]{1,0:T(4,128)S(1)} %collective-permute-done.3.refs_0_), channel_id=1, source_target_pairs={{0,4},{4,0},{8,12},{12,8},{16,20},{20,16},{24,28},{28,24},{1,5},{5... | collective-permute-start | bytes 1677320 | tf_op jit(solution)/shard_map/ppermute | solution.py:39
  65.7 19.4 %collective-permute-start.7 = (f32[4,34944]{1,0:T(4,128)S(1)}, f32[4,34944]{1,0:T(4,128)S(1)}, u32[]{:S(2)}, u32[]{:S(2)}) collective-permute-start(f32[4,34944]{1,0:T(4,128)S(1)} %collective-permute-done.3.refs_0_), channel_id=1, source_target_pairs={{0,8},{4,12},{8,0},{12,4},{16,24},{20,28},{24,16},{28,20},{1,9},{5... | collective-permute-start | bytes 1677320 | tf_op jit(solution)/shard_map/ppermute | solution.py:39
  67.0 18.2 %collective-permute-start.6 = (f32[4,34944]{1,0:T(4,128)S(1)}, f32[4,34944]{1,0:T(4,128)S(1)}, u32[]{:S(2)}, u32[]{:S(2)}) collective-permute-start(f32[4,34944]{1,0:T(4,128)S(1)} %collective-permute-done.3.refs_0_), channel_id=1, source_target_pairs={{0,2},{1,3},{2,0},{3,1},{4,6},{5,7},{6,4},{7,5},{8,10},{9,11},{10,... | collective-permute-start | bytes 1677320 | tf_op jit(solution)/shard_map/ppermute | solution.py:39
  67.7 36.4 %collective-permute-start.8 = (f32[4,34944]{1,0:T(4,128)S(1)}, f32[4,34944]{1,0:T(4,128)S(1)}, u32[]{:S(2)}, u32[]{:S(2)}) collective-permute-start(f32[4,34944]{1,0:T(4,128)S(1)} %collective-permute-done.2.refs_0_), channel_id=1, source_target_pairs={{0,8},{4,12},{8,0},{12,4},{16,24},{20,28},{24,16},{28,20},{1,9},{5... | collective-permute-start | bytes 1677320 | tf_op jit(solution)/shard_map/ppermute | solution.py:39
  68.2 55.6 %collective-permute-start.12 = (f32[4,34944]{1,0:T(4,128)S(1)}, f32[4,34944]{1,0:T(4,128)S(1)}, u32[]{:S(2)}, u32[]{:S(2)}) collective-permute-start(f32[4,34944]{1,0:T(4,128)S(1)} %collective-permute-done.4.refs_0_), channel_id=1, source_target_pairs={{0,2},{1,3},{2,0},{3,1},{4,6},{5,7},{6,4},{7,5},{8,10},{9,11},{10,... | collective-permute-start | bytes 1677320 | tf_op jit(solution)/shard_map/ppermute | solution.py:39
  85.2 20.4 %collective-permute-start.10 = (f32[4,34944]{1,0:T(4,128)S(1)}, f32[4,34944]{1,0:T(4,128)S(1)}, u32[]{:S(2)}, u32[]{:S(2)}) collective-permute-start(f32[4,34944]{1,0:T(4,128)S(1)} %collective-permute-done.6.refs_1_), channel_id=1, source_target_pairs={{0,4},{4,0},{8,12},{12,8},{16,20},{20,16},{24,28},{28,24},{1,5},{5... | collective-permute-start | bytes 1677320 | tf_op jit(solution)/shard_map/ppermute | solution.py:39
  86.5 37.3 %collective-permute-start.13 = (f32[4,34944]{1,0:T(4,128)S(1)}, f32[4,34944]{1,0:T(4,128)S(1)}, u32[]{:S(2)}, u32[]{:S(2)}) collective-permute-start(f32[4,34944]{1,0:T(4,128)S(1)} %collective-permute-done.7.refs_2_), channel_id=1, source_target_pairs={{0,2},{1,3},{2,0},{3,1},{4,6},{5,7},{6,4},{7,5},{8,10},{9,11},{10,... | collective-permute-start | bytes 1677320 | tf_op jit(solution)/shard_map/ppermute | solution.py:39
  104.1 18.6 %collective-permute-start.11 = (f32[4,34944]{1,0:T(4,128)S(1)}, f32[4,34944]{1,0:T(4,128)S(1)}, u32[]{:S(2)}, u32[]{:S(2)}) collective-permute-start(f32[4,34944]{1,0:T(4,128)S(1)} %collective-permute-done.7.refs_2_), channel_id=1, source_target_pairs={{0,4},{4,0},{8,12},{12,8},{16,20},{20,16},{24,28},{28,24},{1,5},{5... | collective-permute-start | bytes 1677320 | tf_op jit(solution)/shard_map/ppermute | solution.py:39
  105.1 46.8 %collective-permute-start.14 = (f32[4,34944]{1,0:T(4,128)S(1)}, f32[4,34944]{1,0:T(4,128)S(1)}, u32[]{:S(2)}, u32[]{:S(2)}) collective-permute-start(f32[4,34944]{1,0:T(4,128)S(1)} %collective-permute-done.8.refs_0_), channel_id=1, source_target_pairs={{0,2},{1,3},{2,0},{3,1},{4,6},{5,7},{6,4},{7,5},{8,10},{9,11},{10,... | collective-permute-start | bytes 1677320 | tf_op jit(solution)/shard_map/ppermute | solution.py:39
  122.7 29.2 %collective-permute-start.15 = (f32[4,34944]{1,0:T(4,128)S(1)}, f32[4,34944]{1,0:T(4,128)S(1)}, u32[]{:S(2)}, u32[]{:S(2)}) collective-permute-start(f32[4,34944]{1,0:T(4,128)S(1)} %collective-permute-done.11.refs_2_), channel_id=1, source_target_pairs={{0,2},{1,3},{2,0},{3,1},{4,6},{5,7},{6,4},{7,5},{8,10},{9,11},{10,... | collective-permute-start | bytes 1677320 | tf_op jit(solution)/shard_map/ppermute | solution.py:39
  151.9 28.5 %copy-start.1 = (bf16[2,512,1536]{2,1,0:T(8,128)(2,1)S(1)}, bf16[2,512,1536]{2,1,0:T(8,128)(2,1)}, u32[]{:S(2)}) copy-start(bf16[2,512,1536]{2,1,0:T(8,128)(2,1)} %constant.207.clone.held_ref) | copy-start | bytes 9437188
  186.9 20.3 %collective-permute-start.18 = (f32[2,1,512,1024]{3,2,1,0:T(8,128)}, f32[2,1,512,1024]{3,2,1,0:T(8,128)}, u32[]{:S(2)}, u32[]{:S(2)}) collective-permute-start(f32[2,1,512,1024]{3,2,1,0:T(8,128)} %columns_transform.5.own_ref), channel_id=1, source_target_pairs={{0,1},{1,0},{2,3},{3,2},{4,5},{5,4},{6,7},{7,6},{8,9},{9,8},{10,11... | collective-permute-start | bytes 12582920 | tf_op jit(solution)/shard_map/ppermute | solution.py:39
  199.5 18.1 %collective-permute-start.17 = (f32[2,1,512,1024]{3,2,1,0:T(8,128)}, f32[2,1,512,1024]{3,2,1,0:T(8,128)}, u32[]{:S(2)}, u32[]{:S(2)}) collective-permute-start(f32[2,1,512,1024]{3,2,1,0:T(8,128)} %columns_transform.4.own_ref), channel_id=1, source_target_pairs={{0,1},{1,0},{2,3},{3,2},{4,5},{5,4},{6,7},{7,6},{8,9},{9,8},{10,11... | collective-permute-start | bytes 12582920 | tf_op jit(solution)/shard_map/ppermute | solution.py:39
  206.2 19.1 %collective-permute-start.16 = (f32[2,1,512,1024]{3,2,1,0:T(8,128)}, f32[2,1,512,1024]{3,2,1,0:T(8,128)}, u32[]{:S(2)}, u32[]{:S(2)}) collective-permute-start(f32[2,1,512,1024]{3,2,1,0:T(8,128)} %columns_transform.3.own_ref), channel_id=1, source_target_pairs={{0,1},{1,0},{2,3},{3,2},{4,5},{5,4},{6,7},{7,6},{8,9},{9,8},{10,11... | collective-permute-start | bytes 12582920 | tf_op jit(solution)/shard_map/ppermute | solution.py:39
  207.3 2.8 %copy-start = (bf16[4,512,1536]{2,1,0:T(8,128)(2,1)S(1)}, bf16[4,512,1536]{2,1,0:T(8,128)(2,1)}, u32[]{:S(2)}) copy-start(bf16[4,512,1536]{2,1,0:T(8,128)(2,1)} %constant.208.clone.held_ref) | copy-start | bytes 18874372

commit v2 on v1

--- a/solution.py
+++ b/solution.py
@@ -163,7 +163,8 @@
 def deposit(sources, signs, cells_x, cells_y, residents, base_mesh, after):
     count = len(sources)
     row_bins = cells_y // BIN_ROWS
-    group_bins = row_bins * GROUP
+    column_bins = GROUP if count > 2 else 2 * GROUP
+    group_bins = row_bins * column_bins
     width = sources[0].shape[-1]
     first_start = width - LANES
     arrivals = first_start - residents
@@ -307,10 +308,10 @@
         lax.fori_loop(1, steps, body, 0)
 
     flops = count * width * BIN_ROWS * BIN_COLS * 24
-    out_spec = pl.BlockSpec((3, GROUP * BIN_COLS, cells_y), lambda g: (0, g, 0))
+    out_spec = pl.BlockSpec((3, column_bins * BIN_COLS, cells_y), lambda g: (0, g, 0))
     return pl.pallas_call(
         kernel,
-        grid=(cells_x // (GROUP * BIN_COLS),),
+        grid=(cells_x // (column_bins * BIN_COLS),),
         in_specs=[pl.BlockSpec(memory_space=pltpu.SMEM)]
         + [pl.BlockSpec(memory_space=pltpu.VMEM)] * count
         + [out_spec] * based
@@ -321,7 +322,7 @@
             pltpu.SMEM((count, 4, LANES), jnp.float32),
             pltpu.SemaphoreType.DMA((count,)),
         ],
-        compiler_params=pltpu.CompilerParams(vmem_limit_bytes=10 << 20),
+        compiler_params=pltpu.CompilerParams(vmem_limit_bytes=12 << 20),
         cost_estimate=pl.CostEstimate(
             flops=flops, bytes_accessed=12 * cells_x * cells_y, transcendentals=0
         ),
@@ -344,7 +345,13 @@
     )
     high = table.astype(ml_dtypes.bfloat16)
     low = (table - high.astype(np.float64)).astype(ml_dtypes.bfloat16)
-    return jnp.asarray(np.concatenate([high, high, low], axis=2))
+    return jnp.asarray(np.concatenate([high, low], axis=2))
+
+
+def tripled(held_ref, residue):
+    length = held_ref.shape[1]
+    high = held_ref[residue, :, :length]
+    return jnp.concatenate([high, high, held_ref[residue, :, length:]], axis=1)
 
 
 def phases(k_first, radix, length, total):
@@ -378,7 +385,7 @@
             high, low = split(jnp.concatenate([real, imag], axis=0))
             pieces.append(
                 jnp.dot(
-                    held_ref[residue],
+                    tripled(held_ref, residue),
                     jnp.concatenate([high, low, high], axis=0),
                     preferred_element_type=jnp.float32,
                 )
@@ -426,7 +433,7 @@
             imag = own_real * b + own_imag * a + other_real * e + other_imag * d
             high, low = split(jnp.concatenate([real, imag], axis=1))
             piece = lax.dot_general(
-                held_ref[residue],
+                tripled(held_ref, residue),
                 jnp.concatenate([high, low, high], axis=1),
                 (((1,), (1,)), ((), ())),
                 preferred_element_type=jnp.float32,
@@ -492,7 +499,7 @@
     bin_cells = BIN_ROWS * BIN_COLS
     slot_count = crossing_rows.shape[-1]
     live_slot = lax.iota(jnp.int32, slot_count) < crossing_count.reshape(1)
-    key = bin_key(crossing_rows.reshape(-1), crossing_columns.reshape(-1), cells_x)
+    key = bin_key(crossing_rows, crossing_columns, cells_x).reshape(-1)
     key = jnp.where(live_slot, key, bins * bin_cells)
     outgoing = lax.sort(
         (key, *(jnp.where(live_slot, crossing_strength[i].reshape(-1), 0.0) for i in range(3))),
@@ -501,16 +508,18 @@
     )
     outgoing = jnp.stack([outgoing[0].astype(jnp.float32), *outgoing[1:]])
     arrived = from_behind(outgoing, "gx", 1)
-    key = bin_key(resident_rows.reshape(-1), resident_columns.reshape(-1), cells_x)
+    key = bin_key(resident_rows, resident_columns, cells_x).reshape(-1)
     residents = key.shape[0]
     key, *strength = lax.sort(
         (key, *(resident_strength[i].reshape(-1) for i in range(3))), num_keys=1, is_stable=False
     )
-    bounds = lax.broadcasted_iota(jnp.int32, (LANES, 1), 0) * bin_cells
+    bounds = lax.broadcasted_iota(jnp.int32, (bins + 8, 1), 0) * bin_cells
     starts = jnp.sum((key[None, :] < bounds).astype(jnp.float32), axis=1)
     starts_2 = jnp.sum((arrived[0:1] < bounds.astype(jnp.float32)).astype(jnp.float32), axis=1)
-    largest = jnp.maximum(jnp.max(jnp.abs(resident_strength)), jnp.max(jnp.abs(arrived[1:])))
-    largest = jnp.maximum(largest, 1e-30)
+    starts, starts_2 = (jnp.pad(values, (0, LANES - bins - 8)) for values in (starts, starts_2))
+    largest = jnp.maximum(jnp.abs(strength[0]), jnp.abs(strength[1]))
+    largest = jnp.max(jnp.maximum(largest, jnp.abs(strength[2])))
+    largest = jnp.maximum(jnp.maximum(largest, jnp.max(jnp.abs(arrived[1:]))), 1e-30)
     particles = jnp.concatenate(
         [
             jnp.stack([key.astype(jnp.float32), *strength]),

time: 236 us -> 229 us (0.970)
  Pallas kernels: 170 us -> 165 us
  other arithmetic: 31.2 us -> 28 us
    pallas_call x7, Pallas kernels: 127 us -> 122 us  [deposit(): pl.pallas_call(kernel, grid=(cells_x // (column_bins * BIN_COLS),), in_sp...]
    add x1 -> x2, other arithmetic: 0.14 us -> 3.06 us  [bin_key(): bin_index * (BIN_ROWS * BIN_COLS) + (rows >> 2) * BIN_COLS]
  transfers between devices with their start and end apart: 19 -> 19, of which waited for: 1 -> 1; matrix products, arithmetic and copies ran while one was open for 11% -> 10% of each run, Pallas kernels for 55% -> 54%
where the time goes in v2:
time: 229 us; the launch traced here: 226 us
  Pallas kernels  165 us (72%)
  other arithmetic  28 us (12%)
  starting transfers between devices  22.5 us (10%)
  local copies, waits for them, and re-layouts  4.2 us (2%)
  between operations  3.43 us (1%)
  waiting for transfers between devices  2.37 us (1%)
    pallas_call x7, Pallas kernels, deposit(): pl.pallas_call(kernel, grid=(cells_x // (column_bins * BIN_COLS),), in_sp...  122 us
    pallas_call x3, Pallas kernels, rows_transform(): pl.pallas_call(kernel, grid=(cells_x // block,), in_specs=[pl.BlockSpec(m...  23.1 us
    ppermute x18, starting transfers between devices, flip(): lax.ppermute(value, axis, [(source, source ^ mask) for source in range(co...  20.4 us
    pallas_call x3, Pallas kernels, columns_transform(): pl.pallas_call(kernel, grid=(cells_y // block,), in_specs=[pl.BlockSpec(m...  19.9 us
    sort x1, other arithmetic, particle_shards(): lax.sort((key, *(resident_strength[i].reshape(-1) for i in range(3))), nu...  16.5 us
  transfers between devices with their start and end apart: 19, of which 1 were waited for; matrix products, arithmetic and copies ran while one was open for 10% of the time, Pallas kernels for 54%

profile of v2, /device:TPU:1, one launch (start us, length us, event | category | flops | bytes accessed | tf_op | source)
XLA Modules:
  0.0 225.9 jit_solution(12252341733184201579)
XLA Ops:
  2.2 4.3 %sort.55 = (s32[2048]{0:T(1024)S(1)}, f32[2048]{0:T(1024)S(1)}, f32[2048]{0:T(1024)S(1)}, f32[2048]{0:T(1024)S(1)}) sort(s32[2048]{0:T(1024)S(1)} %fusion.6, f32[2048]{0:T(1024)S(1)} %fusion.5, f32[2048]{0:T(1024)S(1)} %get-tuple-element.66, f32[2048]{0:T(1024)S(1)} %get-tuple-element.65), dimensions={0}, to_apply=%region_1.2 | sort | flops 22528 | bytes 65536 | tf_op jit(solution)/shard_map/sort | solution.py:504
  6.6 2.1 collective-permute-start
  10.6 2.3 %fusion = s32[1,1,32768]{2,1,0:T(1,128)S(1)} fusion(s32[1,1,32768]{2,1,0:T(1,128)} %param.9, s32[1,1,32768]{2,1,0:T(1,128)} %param.10), kind=kLoop, calls=%fused_computation.8 | loop fusion | flops 1015808 | bytes 393216 | tf_op jit(solution)/shard_map/add | solution.py:160
  12.8 16.5 %sort.54 = (s32[32768]{0:T(1024)S(1)}, f32[32768]{0:T(1024)S(1)}, f32[32768]{0:T(1024)S(1)}, f32[32768]{0:T(1024)S(1)}) sort(s32[32768]{0:T(1024)S(1)} %bitcast.45, f32[32768]{0:T(1024)S(1)} %bitcast.47, f32[32768]{0:T(1024)S(1)} %bitcast.48, f32[32768]{0:T(1024)S(1)} %bitcast.46), dimensions={0}, to_apply=%region_0.1 | sort | flops 491520 | bytes 1048576 | tf_op jit(solution)/shard_map/sort | solution.py:513
  34.4 1.4 collective-permute-start.4
  35.8 2.3 %collective-permute-start.3 = (f32[4,34944]{1,0:T(4,128)S(1)}, f32[4,34944]{1,0:T(4,128)S(1)}, u32[]{:S(2)}, u32[]{:S(2)}) collective-permute-start(f32[4,34944]{1,0:T(4,128)S(1)} %maximum_maximum_fusion.refs_0_), channel_id=1, source_target_pairs={{0,16},{4,20},{8,24},{12,28},{16,0},{20,4},{24,8},{28,12},{1,17},{... | collective-permute-start | bytes 1677320 | tf_op jit(solution)/shard_map/ppermute | solution.py:39
  39.4 9.0 %deposit.7.refs_1_.refs_2_ = f32[3,512,1024]{2,1,0:T(8,128)S(1)} custom-call(f32[1]{0:T(128)} %bitcast.31.signs_ref, f32[4,34944]{1,0:T(4,128)S(1)} %maximum_maximum_fusion.refs_0_), custom_call_target="tpu_custom_call" | custom-call | flops 6870269952 | bytes 6291456 | tf_op jit(solution)/shard_map/deposit/pallas_call | solution.py:312
  48.4 2.3 %collective-permute-done.2.refs_0_ = f32[4,34944]{1,0:T(4,128)S(1)} collective-permute-done((f32[4,34944]{1,0:T(4,128)S(1)}, f32[4,34944]{1,0:T(4,128)S(1)}, u32[]{:S(2)}, u32[]{:S(2)}) %collective-permute-start.2) | collective-permute-done | bytes 559136 | tf_op jit(solution)/shard_map/ppermute | solution.py:39
  52.0 9.5 %deposit.8.refs_2_ = f32[3,512,1024]{2,1,0:T(8,128)S(1)} custom-call(f32[1]{0:T(128)} %bitcast.10.signs_ref, f32[4,34944]{1,0:T(4,128)S(1)} %collective-permute-done.1.refs_0_, f32[3,512,1024]{2,1,0:T(8,128)S(1)} %deposit.7.refs_1_.refs_2_, f32[3,512,1024]{2,1,0:T(8,128)S(1)} %deposit.7.refs_1_.refs_2_), custom_call_target="tpu_custom_call" | custom-call | flops 6870269952 | bytes 6291456 | tf_op jit(solution)/shard_map/deposit/pallas_call | solution.py:312
  61.7 1.6 collective-permute-start.7
  64.8 15.4 %deposit.9.refs_3_.refs_2_ = f32[3,512,1024]{2,1,0:T(8,128)S(1)} custom-call(f32[2]{0:T(128)S(1)} %pad_maximum_fusion.7.signs_ref, f32[4,34944]{1,0:T(4,128)S(1)} %collective-permute-done.2.refs_0_, f32[4,34944]{1,0:T(4,128)S(1)} %collective-permute-done.5.refs_1_, f32[3,512,1024]{2,1,0:T(8,128)S(1)} %deposit.8.refs_2_), custom_call_target="tpu_custom_call" | custom-call | flops 13740539904 | bytes 6291456 | tf_op jit(solution)/shard_map/deposit/pallas_call | solution.py:312
  81.7 16.1 %deposit.10.refs_3_.refs_0_ = f32[3,512,1024]{2,1,0:T(8,128)S(1)} custom-call(f32[2]{0:T(128)S(1)} %pad_maximum_fusion.6.signs_ref, f32[4,34944]{1,0:T(4,128)S(1)} %collective-permute-done.3.refs_0_, f32[4,34944]{1,0:T(4,128)S(1)} %collective-permute-done.6.refs_1_, f32[3,512,1024]{2,1,0:T(8,128)S(1)} %deposit.8.refs_2_, ...), custom_call_target="tpu_custom_call" | custom-call | flops 13740539904 | bytes 6291456 | tf_op jit(solution)/shard_map/deposit/pallas_call | solution.py:312
  97.8 1.3 collective-permute-start.11
  99.4 16.3 %deposit.11.refs_4_.refs_1_ = f32[3,512,1024]{2,1,0:T(8,128)S(1)} custom-call(f32[2]{0:T(128)S(1)} %pad_maximum_fusion.6.signs_ref, f32[4,34944]{1,0:T(4,128)S(1)} %collective-permute-done.9.refs_0_, f32[4,34944]{1,0:T(4,128)S(1)} %collective-permute-done.10.refs_1_, f32[3,512,1024]{2,1,0:T(8,128)S(1)} %deposit.9.refs_3_.refs_2_, ...), custom_call_target="tpu_custom_call" | custom-call | flops 13740539904 | bytes 6291456 | tf_op jit(solution)/shard_map/deposit/pallas_call | solution.py:312
  117.0 28.0 %deposit.12.refs_4_.refs_2_ = f32[3,512,1024]{2,1,0:T(8,128)S(1)} custom-call(f32[4]{0:T(128)S(1)} %pad_maximum_fusion.8.signs_ref, f32[4,34944]{1,0:T(4,128)S(1)} %collective-permute-done.4.refs_0_, f32[4,34944]{1,0:T(4,128)S(1)} %collective-permute-done.12.refs_1_, f32[4,34944]{1,0:T(4,128)S(1)} %collective-permute-done.7.refs_2_, ...), custom_call_target="tpu_custom_call" | custom-call | flops 27481079808 | bytes 6291456 | tf_op jit(solution)/shard_map/deposit/pallas_call | solution.py:312
  145.0 28.1 %deposit.13.refs_3_ = f32[3,512,1024]{2,1,0:T(8,128)S(1)} custom-call(f32[4]{0:T(128)S(1)} %pad_maximum_fusion.8.signs_ref, f32[4,34944]{1,0:T(4,128)S(1)} %collective-permute-done.8.refs_0_, f32[4,34944]{1,0:T(4,128)S(1)} %collective-permute-done.14.refs_1_, f32[4,34944]{1,0:T(4,128)S(1)} %collective-permute-done.11.refs_2_, ...), custom_call_target="tpu_custom_call" | custom-call | flops 27481079808 | bytes 6291456 | tf_op jit(solution)/shard_map/deposit/pallas_call | solution.py:312
  173.3 6.6 %columns_transform.5.own_ref = f32[2,1,512,1024]{3,2,1,0:T(8,128)} custom-call(f32[2,4]{1,0:T(2,128)S(1)} %pad_maximum_fusion.5.scalars_ref, f32[2,512,128]{2,1,0:T(8,128)S(1)} %broadcast_in_dim.17.phase_ref, bf16[2,512,1024]{2,1,0:T(8,128)(2,1)S(1)} %copy-done.1, f32[3,512,1024]{2,1,0:T(8,128)S(1)} %deposit.10.refs_3_.refs_0_, ...), custom_call_target="tpu_custom_call" | custom-call | flops 3221225472 | bytes 12582912 | tf_op jit(solution)/shard_map/columns_transform/pallas_call | solution.py:398
  179.8 6.0 %collective-permute-start.18 = (f32[2,1,512,1024]{3,2,1,0:T(8,128)}, f32[2,1,512,1024]{3,2,1,0:T(8,128)}, u32[]{:S(2)}, u32[]{:S(2)}) collective-permute-start(f32[2,1,512,1024]{3,2,1,0:T(8,128)} %columns_transform.5.own_ref), channel_id=1, source_target_pairs={{0,1},{1,0},{2,3},{3,2},{4,5},{5,4},{6,7},{7,6},{8,9},{9,8},{10,11... | collective-permute-start | bytes 12582920 | tf_op jit(solution)/shard_map/ppermute | solution.py:39
  185.8 6.6 %columns_transform.4.own_ref = f32[2,1,512,1024]{3,2,1,0:T(8,128)} custom-call(f32[2,4]{1,0:T(2,128)S(1)} %pad_maximum_fusion.5.scalars_ref, f32[2,512,128]{2,1,0:T(8,128)S(1)} %broadcast_in_dim.17.phase_ref, bf16[2,512,1024]{2,1,0:T(8,128)(2,1)S(1)} %copy-done.1, f32[3,512,1024]{2,1,0:T(8,128)S(1)} %deposit.10.refs_3_.refs_0_, ...), custom_call_target="tpu_custom_call" | custom-call | flops 3221225472 | bytes 12582912 | tf_op jit(solution)/shard_map/columns_transform/pallas_call | solution.py:398
  192.4 6.8 %columns_transform.3.own_ref = f32[2,1,512,1024]{3,2,1,0:T(8,128)} custom-call(f32[2,4]{1,0:T(2,128)S(1)} %pad_maximum_fusion.5.scalars_ref, f32[2,512,128]{2,1,0:T(8,128)S(1)} %broadcast_in_dim.17.phase_ref, bf16[2,512,1024]{2,1,0:T(8,128)(2,1)S(1)} %copy-done.1, f32[3,512,1024]{2,1,0:T(8,128)S(1)} %deposit.10.refs_3_.refs_0_, ...), custom_call_target="tpu_custom_call" | custom-call | flops 3221225472 | bytes 12582912 | tf_op jit(solution)/shard_map/columns_transform/pallas_call | solution.py:398
  200.3 2.2 copy-done
  202.5 7.7 %rows_transform.3.refs_0_ = f32[2,3,1,1024,512]{4,3,2,1,0:T(8,128)} custom-call(f32[4,1024]{1,0:T(4,128)S(1)} %pad_maximum_fusion.1.scalars_ref, bf16[4,512,1024]{2,1,0:T(8,128)(2,1)S(1)} %copy-done, f32[2,1,512,1024]{3,2,1,0:T(8,128)} %columns_transform.5.own_ref, f32[2,1,512,1024]{3,2,1,0:T(8,128)} %collective-permute-done.18.partner_ref), custom_call_target="tpu_custom_call" | custom-call | flops 3221225472 | bytes 12582912 | tf_op jit(solution)/shard_map/rows_transform/pallas_call | solution.py:456
  210.2 7.7 %rows_transform.4.refs_0_ = f32[2,3,1,1024,512]{4,3,2,1,0:T(8,128)} custom-call(f32[4,1024]{1,0:T(4,128)S(1)} %pad_maximum_fusion.1.scalars_ref, bf16[4,512,1024]{2,1,0:T(8,128)(2,1)S(1)} %copy-done, f32[2,1,512,1024]{3,2,1,0:T(8,128)} %columns_transform.4.own_ref, ...), custom_call_target="tpu_custom_call", output_to_operand_aliasing={{}: (4, {})} | custom-call | flops 3221225472 | bytes 12582912 | tf_op jit(solution)/shard_map/rows_transform/pallas_call | solution.py:456
  217.9 7.7 %rows_transform.5 = f32[2,3,1,1024,512]{4,3,2,1,0:T(8,128)} custom-call(f32[4,1024]{1,0:T(4,128)S(1)} %pad_maximum_fusion.1.scalars_ref, bf16[4,512,1024]{2,1,0:T(8,128)(2,1)S(1)} %copy-done, f32[2,1,512,1024]{3,2,1,0:T(8,128)} %columns_transform.3.own_ref, f32[2,1,512,1024]{3,2,1,0:T(8,128)} %collective-permute-done.16.partner_ref, ...), custom_call_target="tpu_custom_call", output_to_operand_aliasing={{}: (4, {})} | custom-call | flops 3221225472 | bytes 12582912 | tf_op jit(solution)/shard_map/rows_transform/pallas_call | solution.py:456
  (68 shorter events, 14.8 us)
Async XLA Ops:
  6.6 25.1 %collective-permute-start = (f32[4,2048]{1,0:T(4,128)S(1)}, f32[4,2048]{1,0:T(4,128)S(1)}, u32[]{:S(2)}, u32[]{:S(2)}) collective-permute-start(f32[4,2048]{1,0:T(4,128)S(1)} %pad_maximum_fusion), channel_id=1, source_target_pairs={{0,4},{4,8},{8,12},{12,16},{16,20},{20,24},{24,28},{28,0},{1,5},{5... | collective-permute-start | bytes 98312 | tf_op jit(solution)/shard_map/ppermute | solution.py:34
  34.4 27.0 %collective-permute-start.4 = (f32[4,34944]{1,0:T(4,128)S(1)}, f32[4,34944]{1,0:T(4,128)S(1)}, u32[]{:S(2)}, u32[]{:S(2)}) collective-permute-start(f32[4,34944]{1,0:T(4,128)S(1)} %maximum_maximum_fusion.refs_0_), channel_id=1, source_target_pairs={{0,8},{4,12},{8,0},{12,4},{16,24},{20,28},{24,16},{28,20},{1,9},{5... | collective-permute-start | bytes 1677320 | tf_op jit(solution)/shard_map/ppermute | solution.py:39
  35.8 25.7 %collective-permute-start.3 = (f32[4,34944]{1,0:T(4,128)S(1)}, f32[4,34944]{1,0:T(4,128)S(1)}, u32[]{:S(2)}, u32[]{:S(2)}) collective-permute-start(f32[4,34944]{1,0:T(4,128)S(1)} %maximum_maximum_fusion.refs_0_), channel_id=1, source_target_pairs={{0,16},{4,20},{8,24},{12,28},{16,0},{20,4},{24,8},{28,12},{1,17},{... | collective-permute-start | bytes 1677320 | tf_op jit(solution)/shard_map/ppermute | solution.py:39
  38.1 12.6 %collective-permute-start.2 = (f32[4,34944]{1,0:T(4,128)S(1)}, f32[4,34944]{1,0:T(4,128)S(1)}, u32[]{:S(2)}, u32[]{:S(2)}) collective-permute-start(f32[4,34944]{1,0:T(4,128)S(1)} %maximum_maximum_fusion.refs_0_), channel_id=1, source_target_pairs={{0,4},{4,0},{8,12},{12,8},{16,20},{20,16},{24,28},{28,24},{1,5},{5... | collective-permute-start | bytes 1677320 | tf_op jit(solution)/shard_map/ppermute | solution.py:39
  38.1 13.8 %collective-permute-start.1 = (f32[4,34944]{1,0:T(4,128)S(1)}, f32[4,34944]{1,0:T(4,128)S(1)}, u32[]{:S(2)}, u32[]{:S(2)}) collective-permute-start(f32[4,34944]{1,0:T(4,128)S(1)} %maximum_maximum_fusion.refs_0_), channel_id=1, source_target_pairs={{0,2},{1,3},{2,0},{3,1},{4,6},{5,7},{6,4},{7,5},{8,10},{9,11},{10,... | collective-permute-start | bytes 1677320 | tf_op jit(solution)/shard_map/ppermute | solution.py:39
  50.7 13.8 %collective-permute-start.5 = (f32[4,34944]{1,0:T(4,128)S(1)}, f32[4,34944]{1,0:T(4,128)S(1)}, u32[]{:S(2)}, u32[]{:S(2)}) collective-permute-start(f32[4,34944]{1,0:T(4,128)S(1)} %collective-permute-done.2.refs_0_), channel_id=1, source_target_pairs={{0,2},{1,3},{2,0},{3,1},{4,6},{5,7},{6,4},{7,5},{8,10},{9,11},{10,... | collective-permute-start | bytes 1677320 | tf_op jit(solution)/shard_map/ppermute | solution.py:39
  61.4 37.7 %collective-permute-start.9 = (f32[4,34944]{1,0:T(4,128)S(1)}, f32[4,34944]{1,0:T(4,128)S(1)}, u32[]{:S(2)}, u32[]{:S(2)}) collective-permute-start(f32[4,34944]{1,0:T(4,128)S(1)} %collective-permute-done.3.refs_0_), channel_id=1, source_target_pairs={{0,4},{4,0},{8,12},{12,8},{16,20},{20,16},{24,28},{28,24},{1,5},{5... | collective-permute-start | bytes 1677320 | tf_op jit(solution)/shard_map/ppermute | solution.py:39
  61.7 18.5 %collective-permute-start.7 = (f32[4,34944]{1,0:T(4,128)S(1)}, f32[4,34944]{1,0:T(4,128)S(1)}, u32[]{:S(2)}, u32[]{:S(2)}) collective-permute-start(f32[4,34944]{1,0:T(4,128)S(1)} %collective-permute-done.3.refs_0_), channel_id=1, source_target_pairs={{0,8},{4,12},{8,0},{12,4},{16,24},{20,28},{24,16},{28,20},{1,9},{5... | collective-permute-start | bytes 1677320 | tf_op jit(solution)/shard_map/ppermute | solution.py:39
  63.3 16.9 %collective-permute-start.6 = (f32[4,34944]{1,0:T(4,128)S(1)}, f32[4,34944]{1,0:T(4,128)S(1)}, u32[]{:S(2)}, u32[]{:S(2)}) collective-permute-start(f32[4,34944]{1,0:T(4,128)S(1)} %collective-permute-done.3.refs_0_), channel_id=1, source_target_pairs={{0,2},{1,3},{2,0},{3,1},{4,6},{5,7},{6,4},{7,5},{8,10},{9,11},{10,... | collective-permute-start | bytes 1677320 | tf_op jit(solution)/shard_map/ppermute | solution.py:39
  64.5 33.3 %collective-permute-start.8 = (f32[4,34944]{1,0:T(4,128)S(1)}, f32[4,34944]{1,0:T(4,128)S(1)}, u32[]{:S(2)}, u32[]{:S(2)}) collective-permute-start(f32[4,34944]{1,0:T(4,128)S(1)} %collective-permute-done.2.refs_0_), channel_id=1, source_target_pairs={{0,8},{4,12},{8,0},{12,4},{16,24},{20,28},{24,16},{28,20},{1,9},{5... | collective-permute-start | bytes 1677320 | tf_op jit(solution)/shard_map/ppermute | solution.py:39
  64.5 52.4 %collective-permute-start.12 = (f32[4,34944]{1,0:T(4,128)S(1)}, f32[4,34944]{1,0:T(4,128)S(1)}, u32[]{:S(2)}, u32[]{:S(2)}) collective-permute-start(f32[4,34944]{1,0:T(4,128)S(1)} %collective-permute-done.4.refs_0_), channel_id=1, source_target_pairs={{0,2},{1,3},{2,0},{3,1},{4,6},{5,7},{6,4},{7,5},{8,10},{9,11},{10,... | collective-permute-start | bytes 1677320 | tf_op jit(solution)/shard_map/ppermute | solution.py:39
  80.2 19.1 %collective-permute-start.10 = (f32[4,34944]{1,0:T(4,128)S(1)}, f32[4,34944]{1,0:T(4,128)S(1)}, u32[]{:S(2)}, u32[]{:S(2)}) collective-permute-start(f32[4,34944]{1,0:T(4,128)S(1)} %collective-permute-done.6.refs_1_), channel_id=1, source_target_pairs={{0,4},{4,0},{8,12},{12,8},{16,20},{20,16},{24,28},{28,24},{1,5},{5... | collective-permute-start | bytes 1677320 | tf_op jit(solution)/shard_map/ppermute | solution.py:39
  81.5 35.5 %collective-permute-start.13 = (f32[4,34944]{1,0:T(4,128)S(1)}, f32[4,34944]{1,0:T(4,128)S(1)}, u32[]{:S(2)}, u32[]{:S(2)}) collective-permute-start(f32[4,34944]{1,0:T(4,128)S(1)} %collective-permute-done.7.refs_2_), channel_id=1, source_target_pairs={{0,2},{1,3},{2,0},{3,1},{4,6},{5,7},{6,4},{7,5},{8,10},{9,11},{10,... | collective-permute-start | bytes 1677320 | tf_op jit(solution)/shard_map/ppermute | solution.py:39
  97.8 17.8 %collective-permute-start.11 = (f32[4,34944]{1,0:T(4,128)S(1)}, f32[4,34944]{1,0:T(4,128)S(1)}, u32[]{:S(2)}, u32[]{:S(2)}) collective-permute-start(f32[4,34944]{1,0:T(4,128)S(1)} %collective-permute-done.7.refs_2_), channel_id=1, source_target_pairs={{0,4},{4,0},{8,12},{12,8},{16,20},{20,16},{24,28},{28,24},{1,5},{5... | collective-permute-start | bytes 1677320 | tf_op jit(solution)/shard_map/ppermute | solution.py:39
  99.2 45.8 %collective-permute-start.14 = (f32[4,34944]{1,0:T(4,128)S(1)}, f32[4,34944]{1,0:T(4,128)S(1)}, u32[]{:S(2)}, u32[]{:S(2)}) collective-permute-start(f32[4,34944]{1,0:T(4,128)S(1)} %collective-permute-done.8.refs_0_), channel_id=1, source_target_pairs={{0,2},{1,3},{2,0},{3,1},{4,6},{5,7},{6,4},{7,5},{8,10},{9,11},{10,... | collective-permute-start | bytes 1677320 | tf_op jit(solution)/shard_map/ppermute | solution.py:39
  115.7 29.3 %collective-permute-start.15 = (f32[4,34944]{1,0:T(4,128)S(1)}, f32[4,34944]{1,0:T(4,128)S(1)}, u32[]{:S(2)}, u32[]{:S(2)}) collective-permute-start(f32[4,34944]{1,0:T(4,128)S(1)} %collective-permute-done.11.refs_2_), channel_id=1, source_target_pairs={{0,2},{1,3},{2,0},{3,1},{4,6},{5,7},{6,4},{7,5},{8,10},{9,11},{10,... | collective-permute-start | bytes 1677320 | tf_op jit(solution)/shard_map/ppermute | solution.py:39
  145.0 28.3 %copy-start.1 = (bf16[2,512,1024]{2,1,0:T(8,128)(2,1)S(1)}, bf16[2,512,1024]{2,1,0:T(8,128)(2,1)}, u32[]{:S(2)}) copy-start(bf16[2,512,1024]{2,1,0:T(8,128)(2,1)} %constant.208.clone.held_ref) | copy-start | bytes 6291460
  179.8 20.4 %collective-permute-start.18 = (f32[2,1,512,1024]{3,2,1,0:T(8,128)}, f32[2,1,512,1024]{3,2,1,0:T(8,128)}, u32[]{:S(2)}, u32[]{:S(2)}) collective-permute-start(f32[2,1,512,1024]{3,2,1,0:T(8,128)} %columns_transform.5.own_ref), channel_id=1, source_target_pairs={{0,1},{1,0},{2,3},{3,2},{4,5},{5,4},{6,7},{7,6},{8,9},{9,8},{10,11... | collective-permute-start | bytes 12582920 | tf_op jit(solution)/shard_map/ppermute | solution.py:39
  192.4 17.7 %collective-permute-start.17 = (f32[2,1,512,1024]{3,2,1,0:T(8,128)}, f32[2,1,512,1024]{3,2,1,0:T(8,128)}, u32[]{:S(2)}, u32[]{:S(2)}) collective-permute-start(f32[2,1,512,1024]{3,2,1,0:T(8,128)} %columns_transform.4.own_ref), channel_id=1, source_target_pairs={{0,1},{1,0},{2,3},{3,2},{4,5},{5,4},{6,7},{7,6},{8,9},{9,8},{10,11... | collective-permute-start | bytes 12582920 | tf_op jit(solution)/shard_map/ppermute | solution.py:39
  199.2 18.7 %collective-permute-start.16 = (f32[2,1,512,1024]{3,2,1,0:T(8,128)}, f32[2,1,512,1024]{3,2,1,0:T(8,128)}, u32[]{:S(2)}, u32[]{:S(2)}) collective-permute-start(f32[2,1,512,1024]{3,2,1,0:T(8,128)} %columns_transform.3.own_ref), channel_id=1, source_target_pairs={{0,1},{1,0},{2,3},{3,2},{4,5},{5,4},{6,7},{7,6},{8,9},{9,8},{10,11... | collective-permute-start | bytes 12582920 | tf_op jit(solution)/shard_map/ppermute | solution.py:39
  200.3 2.2 copy-start

commit v3 on v2

--- a/solution.py
+++ b/solution.py
@@ -19,7 +19,7 @@
 BIN_ROWS = 256
 BIN_COLS = 32
 CHUNK = 640
-GROUP = 2
+GROUP = 4
 
 F8 = jnp.float8_e4m3fn
 PIECES = 3
@@ -163,7 +163,7 @@
 def deposit(sources, signs, cells_x, cells_y, residents, base_mesh, after):
     count = len(sources)
     row_bins = cells_y // BIN_ROWS
-    column_bins = GROUP if count > 2 else 2 * GROUP
+    column_bins = GROUP
     group_bins = row_bins * column_bins
     width = sources[0].shape[-1]
     first_start = width - LANES

time: 229 us -> 226 us (0.987)
  transfers between devices with their start and end apart: 19 -> 19, of which waited for: 1 -> 1; matrix products, arithmetic and copies ran while one was open for 10% -> 10% of each run, Pallas kernels for 54% -> 55%
where the time goes in v3:
time: 226 us; the launch traced here: 223 us
  Pallas kernels  163 us (72%)
  other arithmetic  27.8 us (12%)
  starting transfers between devices  22.5 us (10%)
  local copies, waits for them, and re-layouts  4.2 us (2%)
  between operations  3.39 us (2%)
    pallas_call x7, Pallas kernels, deposit(): pl.pallas_call(kernel, grid=(cells_x // (column_bins * BIN_COLS),), in_sp...  120 us
    pallas_call x3, Pallas kernels, rows_transform(): pl.pallas_call(kernel, grid=(cells_x // block,), in_specs=[pl.BlockSpec(m...  23.1 us
    ppermute x18, starting transfers between devices, flip(): lax.ppermute(value, axis, [(source, source ^ mask) for source in range(co...  20.4 us
    pallas_call x3, Pallas kernels, columns_transform(): pl.pallas_call(kernel, grid=(cells_y // block,), in_specs=[pl.BlockSpec(m...  19.7 us
    sort x1, other arithmetic, particle_shards(): lax.sort((key, *(resident_strength[i].reshape(-1) for i in range(3))), nu...  16.3 us
  transfers between devices with their start and end apart: 19, of which 1 were waited for; matrix products, arithmetic and copies ran while one was open for 10% of the time, Pallas kernels for 55%

profile of v3, /device:TPU:1, one launch (start us, length us, event | category | flops | bytes accessed | tf_op | source)
XLA Modules:
  0.0 223.1 jit_solution(2969623801211429845)
XLA Ops:
  2.2 4.3 %sort.55 = (s32[2048]{0:T(1024)S(1)}, f32[2048]{0:T(1024)S(1)}, f32[2048]{0:T(1024)S(1)}, f32[2048]{0:T(1024)S(1)}) sort(s32[2048]{0:T(1024)S(1)} %fusion.6, f32[2048]{0:T(1024)S(1)} %fusion.5, f32[2048]{0:T(1024)S(1)} %get-tuple-element.66, f32[2048]{0:T(1024)S(1)} %get-tuple-element.65), dimensions={0}, to_apply=%region_1.2 | sort | flops 22528 | bytes 65536 | tf_op jit(solution)/shard_map/sort | solution.py:504
  6.6 2.1 collective-permute-start
  10.6 2.3 %fusion = s32[1,1,32768]{2,1,0:T(1,128)S(1)} fusion(s32[1,1,32768]{2,1,0:T(1,128)} %param.9, s32[1,1,32768]{2,1,0:T(1,128)} %param.10), kind=kLoop, calls=%fused_computation.8 | loop fusion | flops 1015808 | bytes 393216 | tf_op jit(solution)/shard_map/add | solution.py:160
  12.8 16.3 %sort.54 = (s32[32768]{0:T(1024)S(1)}, f32[32768]{0:T(1024)S(1)}, f32[32768]{0:T(1024)S(1)}, f32[32768]{0:T(1024)S(1)}) sort(s32[32768]{0:T(1024)S(1)} %bitcast.45, f32[32768]{0:T(1024)S(1)} %bitcast.47, f32[32768]{0:T(1024)S(1)} %bitcast.48, f32[32768]{0:T(1024)S(1)} %bitcast.46), dimensions={0}, to_apply=%region_0.1 | sort | flops 491520 | bytes 1048576 | tf_op jit(solution)/shard_map/sort | solution.py:513
  34.2 1.4 collective-permute-start.4
  35.5 2.3 %collective-permute-start.3 = (f32[4,34944]{1,0:T(4,128)S(1)}, f32[4,34944]{1,0:T(4,128)S(1)}, u32[]{:S(2)}, u32[]{:S(2)}) collective-permute-start(f32[4,34944]{1,0:T(4,128)S(1)} %maximum_maximum_fusion.refs_0_), channel_id=1, source_target_pairs={{0,16},{4,20},{8,24},{12,28},{16,0},{20,4},{24,8},{28,12},{1,17},{... | collective-permute-start | bytes 1677320 | tf_op jit(solution)/shard_map/ppermute | solution.py:39
  39.1 9.4 %deposit.7.refs_1_.refs_2_ = f32[3,512,1024]{2,1,0:T(8,128)S(1)} custom-call(f32[1]{0:T(128)} %bitcast.31.signs_ref, f32[4,34944]{1,0:T(4,128)S(1)} %maximum_maximum_fusion.refs_0_), custom_call_target="tpu_custom_call" | custom-call | flops 6870269952 | bytes 6291456 | tf_op jit(solution)/shard_map/deposit/pallas_call | solution.py:312
  48.5 2.0 collective-permute-done.2.refs_0_
  51.7 9.4 %deposit.8.refs_2_ = f32[3,512,1024]{2,1,0:T(8,128)S(1)} custom-call(f32[1]{0:T(128)} %bitcast.10.signs_ref, f32[4,34944]{1,0:T(4,128)S(1)} %collective-permute-done.1.refs_0_, f32[3,512,1024]{2,1,0:T(8,128)S(1)} %deposit.7.refs_1_.refs_2_, f32[3,512,1024]{2,1,0:T(8,128)S(1)} %deposit.7.refs_1_.refs_2_), custom_call_target="tpu_custom_call" | custom-call | flops 6870269952 | bytes 6291456 | tf_op jit(solution)/shard_map/deposit/pallas_call | solution.py:312
  61.5 1.6 collective-permute-start.7
  64.5 15.4 %deposit.9.refs_3_.refs_2_ = f32[3,512,1024]{2,1,0:T(8,128)S(1)} custom-call(f32[2]{0:T(128)S(1)} %pad_maximum_fusion.7.signs_ref, f32[4,34944]{1,0:T(4,128)S(1)} %collective-permute-done.2.refs_0_, f32[4,34944]{1,0:T(4,128)S(1)} %collective-permute-done.5.refs_1_, f32[3,512,1024]{2,1,0:T(8,128)S(1)} %deposit.8.refs_2_), custom_call_target="tpu_custom_call" | custom-call | flops 13740539904 | bytes 6291456 | tf_op jit(solution)/shard_map/deposit/pallas_call | solution.py:312
  81.5 16.0 %deposit.10.refs_3_.refs_0_ = f32[3,512,1024]{2,1,0:T(8,128)S(1)} custom-call(f32[2]{0:T(128)S(1)} %pad_maximum_fusion.6.signs_ref, f32[4,34944]{1,0:T(4,128)S(1)} %collective-permute-done.3.refs_0_, f32[4,34944]{1,0:T(4,128)S(1)} %collective-permute-done.6.refs_1_, f32[3,512,1024]{2,1,0:T(8,128)S(1)} %deposit.8.refs_2_, ...), custom_call_target="tpu_custom_call" | custom-call | flops 13740539904 | bytes 6291456 | tf_op jit(solution)/shard_map/deposit/pallas_call | solution.py:312
  97.5 1.3 collective-permute-start.11
  99.1 16.1 %deposit.11.refs_4_.refs_1_ = f32[3,512,1024]{2,1,0:T(8,128)S(1)} custom-call(f32[2]{0:T(128)S(1)} %pad_maximum_fusion.6.signs_ref, f32[4,34944]{1,0:T(4,128)S(1)} %collective-permute-done.9.refs_0_, f32[4,34944]{1,0:T(4,128)S(1)} %collective-permute-done.10.refs_1_, f32[3,512,1024]{2,1,0:T(8,128)S(1)} %deposit.9.refs_3_.refs_2_, ...), custom_call_target="tpu_custom_call" | custom-call | flops 13740539904 | bytes 6291456 | tf_op jit(solution)/shard_map/deposit/pallas_call | solution.py:312
  116.5 27.1 %deposit.12.refs_4_.refs_2_ = f32[3,512,1024]{2,1,0:T(8,128)S(1)} custom-call(f32[4]{0:T(128)S(1)} %pad_maximum_fusion.8.signs_ref, f32[4,34944]{1,0:T(4,128)S(1)} %collective-permute-done.4.refs_0_, f32[4,34944]{1,0:T(4,128)S(1)} %collective-permute-done.12.refs_1_, f32[4,34944]{1,0:T(4,128)S(1)} %collective-permute-done.7.refs_2_, ...), custom_call_target="tpu_custom_call" | custom-call | flops 27481079808 | bytes 6291456 | tf_op jit(solution)/shard_map/deposit/pallas_call | solution.py:312
  143.6 27.0 %deposit.13.refs_3_ = f32[3,512,1024]{2,1,0:T(8,128)S(1)} custom-call(f32[4]{0:T(128)S(1)} %pad_maximum_fusion.8.signs_ref, f32[4,34944]{1,0:T(4,128)S(1)} %collective-permute-done.8.refs_0_, f32[4,34944]{1,0:T(4,128)S(1)} %collective-permute-done.14.refs_1_, f32[4,34944]{1,0:T(4,128)S(1)} %collective-permute-done.11.refs_2_, ...), custom_call_target="tpu_custom_call" | custom-call | flops 27481079808 | bytes 6291456 | tf_op jit(solution)/shard_map/deposit/pallas_call | solution.py:312
  170.8 6.6 %columns_transform.5.own_ref = f32[2,1,512,1024]{3,2,1,0:T(8,128)} custom-call(f32[2,4]{1,0:T(2,128)S(1)} %pad_maximum_fusion.5.scalars_ref, f32[2,512,128]{2,1,0:T(8,128)S(1)} %broadcast_in_dim.17.phase_ref, bf16[2,512,1024]{2,1,0:T(8,128)(2,1)S(1)} %copy-done.1, f32[3,512,1024]{2,1,0:T(8,128)S(1)} %deposit.10.refs_3_.refs_0_, ...), custom_call_target="tpu_custom_call" | custom-call | flops 3221225472 | bytes 12582912 | tf_op jit(solution)/shard_map/columns_transform/pallas_call | solution.py:398
  177.4 6.0 %collective-permute-start.18 = (f32[2,1,512,1024]{3,2,1,0:T(8,128)}, f32[2,1,512,1024]{3,2,1,0:T(8,128)}, u32[]{:S(2)}, u32[]{:S(2)}) collective-permute-start(f32[2,1,512,1024]{3,2,1,0:T(8,128)} %columns_transform.5.own_ref), channel_id=1, source_target_pairs={{0,1},{1,0},{2,3},{3,2},{4,5},{5,4},{6,7},{7,6},{8,9},{9,8},{10,11... | collective-permute-start | bytes 12582920 | tf_op jit(solution)/shard_map/ppermute | solution.py:39
  183.4 6.6 %columns_transform.4.own_ref = f32[2,1,512,1024]{3,2,1,0:T(8,128)} custom-call(f32[2,4]{1,0:T(2,128)S(1)} %pad_maximum_fusion.5.scalars_ref, f32[2,512,128]{2,1,0:T(8,128)S(1)} %broadcast_in_dim.17.phase_ref, bf16[2,512,1024]{2,1,0:T(8,128)(2,1)S(1)} %copy-done.1, f32[3,512,1024]{2,1,0:T(8,128)S(1)} %deposit.10.refs_3_.refs_0_, ...), custom_call_target="tpu_custom_call" | custom-call | flops 3221225472 | bytes 12582912 | tf_op jit(solution)/shard_map/columns_transform/pallas_call | solution.py:398
  190.0 6.5 %columns_transform.3.own_ref = f32[2,1,512,1024]{3,2,1,0:T(8,128)} custom-call(f32[2,4]{1,0:T(2,128)S(1)} %pad_maximum_fusion.5.scalars_ref, f32[2,512,128]{2,1,0:T(8,128)S(1)} %broadcast_in_dim.17.phase_ref, bf16[2,512,1024]{2,1,0:T(8,128)(2,1)S(1)} %copy-done.1, f32[3,512,1024]{2,1,0:T(8,128)S(1)} %deposit.10.refs_3_.refs_0_, ...), custom_call_target="tpu_custom_call" | custom-call | flops 3221225472 | bytes 12582912 | tf_op jit(solution)/shard_map/columns_transform/pallas_call | solution.py:398
  197.6 2.2 copy-done
  199.8 7.7 %rows_transform.3.refs_0_ = f32[2,3,1,1024,512]{4,3,2,1,0:T(8,128)} custom-call(f32[4,1024]{1,0:T(4,128)S(1)} %pad_maximum_fusion.1.scalars_ref, bf16[4,512,1024]{2,1,0:T(8,128)(2,1)S(1)} %copy-done, f32[2,1,512,1024]{3,2,1,0:T(8,128)} %columns_transform.5.own_ref, f32[2,1,512,1024]{3,2,1,0:T(8,128)} %collective-permute-done.18.partner_ref), custom_call_target="tpu_custom_call" | custom-call | flops 3221225472 | bytes 12582912 | tf_op jit(solution)/shard_map/rows_transform/pallas_call | solution.py:456
  207.5 7.7 %rows_transform.4.refs_0_ = f32[2,3,1,1024,512]{4,3,2,1,0:T(8,128)} custom-call(f32[4,1024]{1,0:T(4,128)S(1)} %pad_maximum_fusion.1.scalars_ref, bf16[4,512,1024]{2,1,0:T(8,128)(2,1)S(1)} %copy-done, f32[2,1,512,1024]{3,2,1,0:T(8,128)} %columns_transform.4.own_ref, ...), custom_call_target="tpu_custom_call", output_to_operand_aliasing={{}: (4, {})} | custom-call | flops 3221225472 | bytes 12582912 | tf_op jit(solution)/shard_map/rows_transform/pallas_call | solution.py:456
  215.2 7.7 %rows_transform.5 = f32[2,3,1,1024,512]{4,3,2,1,0:T(8,128)} custom-call(f32[4,1024]{1,0:T(4,128)S(1)} %pad_maximum_fusion.1.scalars_ref, bf16[4,512,1024]{2,1,0:T(8,128)(2,1)S(1)} %copy-done, f32[2,1,512,1024]{3,2,1,0:T(8,128)} %columns_transform.3.own_ref, f32[2,1,512,1024]{3,2,1,0:T(8,128)} %collective-permute-done.16.partner_ref, ...), custom_call_target="tpu_custom_call", output_to_operand_aliasing={{}: (4, {})} | custom-call | flops 3221225472 | bytes 12582912 | tf_op jit(solution)/shard_map/rows_transform/pallas_call | solution.py:456
  (68 shorter events, 14.8 us)
Async XLA Ops:
  6.6 24.9 %collective-permute-start = (f32[4,2048]{1,0:T(4,128)S(1)}, f32[4,2048]{1,0:T(4,128)S(1)}, u32[]{:S(2)}, u32[]{:S(2)}) collective-permute-start(f32[4,2048]{1,0:T(4,128)S(1)} %pad_maximum_fusion), channel_id=1, source_target_pairs={{0,4},{4,8},{8,12},{12,16},{16,20},{20,24},{24,28},{28,0},{1,5},{5... | collective-permute-start | bytes 98312 | tf_op jit(solution)/shard_map/ppermute | solution.py:34
  34.2 27.0 %collective-permute-start.4 = (f32[4,34944]{1,0:T(4,128)S(1)}, f32[4,34944]{1,0:T(4,128)S(1)}, u32[]{:S(2)}, u32[]{:S(2)}) collective-permute-start(f32[4,34944]{1,0:T(4,128)S(1)} %maximum_maximum_fusion.refs_0_), channel_id=1, source_target_pairs={{0,8},{4,12},{8,0},{12,4},{16,24},{20,28},{24,16},{28,20},{1,9},{5... | collective-permute-start | bytes 1677320 | tf_op jit(solution)/shard_map/ppermute | solution.py:39
  35.5 25.7 %collective-permute-start.3 = (f32[4,34944]{1,0:T(4,128)S(1)}, f32[4,34944]{1,0:T(4,128)S(1)}, u32[]{:S(2)}, u32[]{:S(2)}) collective-permute-start(f32[4,34944]{1,0:T(4,128)S(1)} %maximum_maximum_fusion.refs_0_), channel_id=1, source_target_pairs={{0,16},{4,20},{8,24},{12,28},{16,0},{20,4},{24,8},{28,12},{1,17},{... | collective-permute-start | bytes 1677320 | tf_op jit(solution)/shard_map/ppermute | solution.py:39
  37.8 12.6 %collective-permute-start.2 = (f32[4,34944]{1,0:T(4,128)S(1)}, f32[4,34944]{1,0:T(4,128)S(1)}, u32[]{:S(2)}, u32[]{:S(2)}) collective-permute-start(f32[4,34944]{1,0:T(4,128)S(1)} %maximum_maximum_fusion.refs_0_), channel_id=1, source_target_pairs={{0,4},{4,0},{8,12},{12,8},{16,20},{20,16},{24,28},{28,24},{1,5},{5... | collective-permute-start | bytes 1677320 | tf_op jit(solution)/shard_map/ppermute | solution.py:39
  37.9 13.8 %collective-permute-start.1 = (f32[4,34944]{1,0:T(4,128)S(1)}, f32[4,34944]{1,0:T(4,128)S(1)}, u32[]{:S(2)}, u32[]{:S(2)}) collective-permute-start(f32[4,34944]{1,0:T(4,128)S(1)} %maximum_maximum_fusion.refs_0_), channel_id=1, source_target_pairs={{0,2},{1,3},{2,0},{3,1},{4,6},{5,7},{6,4},{7,5},{8,10},{9,11},{10,... | collective-permute-start | bytes 1677320 | tf_op jit(solution)/shard_map/ppermute | solution.py:39
  50.5 13.8 %collective-permute-start.5 = (f32[4,34944]{1,0:T(4,128)S(1)}, f32[4,34944]{1,0:T(4,128)S(1)}, u32[]{:S(2)}, u32[]{:S(2)}) collective-permute-start(f32[4,34944]{1,0:T(4,128)S(1)} %collective-permute-done.2.refs_0_), channel_id=1, source_target_pairs={{0,2},{1,3},{2,0},{3,1},{4,6},{5,7},{6,4},{7,5},{8,10},{9,11},{10,... | collective-permute-start | bytes 1677320 | tf_op jit(solution)/shard_map/ppermute | solution.py:39
  61.2 37.6 %collective-permute-start.9 = (f32[4,34944]{1,0:T(4,128)S(1)}, f32[4,34944]{1,0:T(4,128)S(1)}, u32[]{:S(2)}, u32[]{:S(2)}) collective-permute-start(f32[4,34944]{1,0:T(4,128)S(1)} %collective-permute-done.3.refs_0_), channel_id=1, source_target_pairs={{0,4},{4,0},{8,12},{12,8},{16,20},{20,16},{24,28},{28,24},{1,5},{5... | collective-permute-start | bytes 1677320 | tf_op jit(solution)/shard_map/ppermute | solution.py:39
  61.5 18.5 %collective-permute-start.7 = (f32[4,34944]{1,0:T(4,128)S(1)}, f32[4,34944]{1,0:T(4,128)S(1)}, u32[]{:S(2)}, u32[]{:S(2)}) collective-permute-start(f32[4,34944]{1,0:T(4,128)S(1)} %collective-permute-done.3.refs_0_), channel_id=1, source_target_pairs={{0,8},{4,12},{8,0},{12,4},{16,24},{20,28},{24,16},{28,20},{1,9},{5... | collective-permute-start | bytes 1677320 | tf_op jit(solution)/shard_map/ppermute | solution.py:39
  63.1 16.9 %collective-permute-start.6 = (f32[4,34944]{1,0:T(4,128)S(1)}, f32[4,34944]{1,0:T(4,128)S(1)}, u32[]{:S(2)}, u32[]{:S(2)}) collective-permute-start(f32[4,34944]{1,0:T(4,128)S(1)} %collective-permute-done.3.refs_0_), channel_id=1, source_target_pairs={{0,2},{1,3},{2,0},{3,1},{4,6},{5,7},{6,4},{7,5},{8,10},{9,11},{10,... | collective-permute-start | bytes 1677320 | tf_op jit(solution)/shard_map/ppermute | solution.py:39
  64.3 33.2 %collective-permute-start.8 = (f32[4,34944]{1,0:T(4,128)S(1)}, f32[4,34944]{1,0:T(4,128)S(1)}, u32[]{:S(2)}, u32[]{:S(2)}) collective-permute-start(f32[4,34944]{1,0:T(4,128)S(1)} %collective-permute-done.2.refs_0_), channel_id=1, source_target_pairs={{0,8},{4,12},{8,0},{12,4},{16,24},{20,28},{24,16},{28,20},{1,9},{5... | collective-permute-start | bytes 1677320 | tf_op jit(solution)/shard_map/ppermute | solution.py:39
  64.3 52.2 %collective-permute-start.12 = (f32[4,34944]{1,0:T(4,128)S(1)}, f32[4,34944]{1,0:T(4,128)S(1)}, u32[]{:S(2)}, u32[]{:S(2)}) collective-permute-start(f32[4,34944]{1,0:T(4,128)S(1)} %collective-permute-done.4.refs_0_), channel_id=1, source_target_pairs={{0,2},{1,3},{2,0},{3,1},{4,6},{5,7},{6,4},{7,5},{8,10},{9,11},{10,... | collective-permute-start | bytes 1677320 | tf_op jit(solution)/shard_map/ppermute | solution.py:39
  80.0 19.1 %collective-permute-start.10 = (f32[4,34944]{1,0:T(4,128)S(1)}, f32[4,34944]{1,0:T(4,128)S(1)}, u32[]{:S(2)}, u32[]{:S(2)}) collective-permute-start(f32[4,34944]{1,0:T(4,128)S(1)} %collective-permute-done.6.refs_1_), channel_id=1, source_target_pairs={{0,4},{4,0},{8,12},{12,8},{16,20},{20,16},{24,28},{28,24},{1,5},{5... | collective-permute-start | bytes 1677320 | tf_op jit(solution)/shard_map/ppermute | solution.py:39
  81.2 35.3 %collective-permute-start.13 = (f32[4,34944]{1,0:T(4,128)S(1)}, f32[4,34944]{1,0:T(4,128)S(1)}, u32[]{:S(2)}, u32[]{:S(2)}) collective-permute-start(f32[4,34944]{1,0:T(4,128)S(1)} %collective-permute-done.7.refs_2_), channel_id=1, source_target_pairs={{0,2},{1,3},{2,0},{3,1},{4,6},{5,7},{6,4},{7,5},{8,10},{9,11},{10,... | collective-permute-start | bytes 1677320 | tf_op jit(solution)/shard_map/ppermute | solution.py:39
  97.5 17.6 %collective-permute-start.11 = (f32[4,34944]{1,0:T(4,128)S(1)}, f32[4,34944]{1,0:T(4,128)S(1)}, u32[]{:S(2)}, u32[]{:S(2)}) collective-permute-start(f32[4,34944]{1,0:T(4,128)S(1)} %collective-permute-done.7.refs_2_), channel_id=1, source_target_pairs={{0,4},{4,0},{8,12},{12,8},{16,20},{20,16},{24,28},{28,24},{1,5},{5... | collective-permute-start | bytes 1677320 | tf_op jit(solution)/shard_map/ppermute | solution.py:39
  98.8 44.7 %collective-permute-start.14 = (f32[4,34944]{1,0:T(4,128)S(1)}, f32[4,34944]{1,0:T(4,128)S(1)}, u32[]{:S(2)}, u32[]{:S(2)}) collective-permute-start(f32[4,34944]{1,0:T(4,128)S(1)} %collective-permute-done.8.refs_0_), channel_id=1, source_target_pairs={{0,2},{1,3},{2,0},{3,1},{4,6},{5,7},{6,4},{7,5},{8,10},{9,11},{10,... | collective-permute-start | bytes 1677320 | tf_op jit(solution)/shard_map/ppermute | solution.py:39
  115.1 28.4 %collective-permute-start.15 = (f32[4,34944]{1,0:T(4,128)S(1)}, f32[4,34944]{1,0:T(4,128)S(1)}, u32[]{:S(2)}, u32[]{:S(2)}) collective-permute-start(f32[4,34944]{1,0:T(4,128)S(1)} %collective-permute-done.11.refs_2_), channel_id=1, source_target_pairs={{0,2},{1,3},{2,0},{3,1},{4,6},{5,7},{6,4},{7,5},{8,10},{9,11},{10,... | collective-permute-start | bytes 1677320 | tf_op jit(solution)/shard_map/ppermute | solution.py:39
  143.5 27.3 %copy-start.1 = (bf16[2,512,1024]{2,1,0:T(8,128)(2,1)S(1)}, bf16[2,512,1024]{2,1,0:T(8,128)(2,1)}, u32[]{:S(2)}) copy-start(bf16[2,512,1024]{2,1,0:T(8,128)(2,1)} %constant.208.clone.held_ref) | copy-start | bytes 6291460
  177.4 20.2 %collective-permute-start.18 = (f32[2,1,512,1024]{3,2,1,0:T(8,128)}, f32[2,1,512,1024]{3,2,1,0:T(8,128)}, u32[]{:S(2)}, u32[]{:S(2)}) collective-permute-start(f32[2,1,512,1024]{3,2,1,0:T(8,128)} %columns_transform.5.own_ref), channel_id=1, source_target_pairs={{0,1},{1,0},{2,3},{3,2},{4,5},{5,4},{6,7},{7,6},{8,9},{9,8},{10,11... | collective-permute-start | bytes 12582920 | tf_op jit(solution)/shard_map/ppermute | solution.py:39
  190.0 17.5 %collective-permute-start.17 = (f32[2,1,512,1024]{3,2,1,0:T(8,128)}, f32[2,1,512,1024]{3,2,1,0:T(8,128)}, u32[]{:S(2)}, u32[]{:S(2)}) collective-permute-start(f32[2,1,512,1024]{3,2,1,0:T(8,128)} %columns_transform.4.own_ref), channel_id=1, source_target_pairs={{0,1},{1,0},{2,3},{3,2},{4,5},{5,4},{6,7},{7,6},{8,9},{9,8},{10,11... | collective-permute-start | bytes 12582920 | tf_op jit(solution)/shard_map/ppermute | solution.py:39
  196.5 18.7 %collective-permute-start.16 = (f32[2,1,512,1024]{3,2,1,0:T(8,128)}, f32[2,1,512,1024]{3,2,1,0:T(8,128)}, u32[]{:S(2)}, u32[]{:S(2)}) collective-permute-start(f32[2,1,512,1024]{3,2,1,0:T(8,128)} %columns_transform.3.own_ref), channel_id=1, source_target_pairs={{0,1},{1,0},{2,3},{3,2},{4,5},{5,4},{6,7},{7,6},{8,9},{9,8},{10,11... | collective-permute-start | bytes 12582920 | tf_op jit(solution)/shard_map/ppermute | solution.py:39
  197.6 2.2 copy-start
